TPU v7x, 256 devices: a whole 4x4x8 slice. The times are simulated.
256 devices in a mesh: frame: 2 (over x_lo), tile: 128 (over z, y, x_hi, core).
Axes of the slice: x: 4 (x_hi: 2, x_lo: 2; x = x_hi * 2 + x_lo), y: 4, z: 8, core: 2. Of those that a mesh axis runs over, the one named last changes fastest.
Arguments:
- tokens: bfloat16 [4, 24576, 1024], P('frame', 'tile'), may hold values from -6 to 6
- norm_gain: float32 [1024], replicated, may hold values from 0.1 to 1.9
- modulation: float32 [4, 1024], P('frame'), may hold values from -1.5 to 6
- w_query: bfloat16 [1024, 1024], replicated, may hold values from -0.1875 to 0.1875
- w_key: bfloat16 [1024, 1024], replicated, may hold values from -0.1875 to 0.1875
- w_value: bfloat16 [1024, 1024], replicated, may hold values from -0.1875 to 0.1875
- w_out: bfloat16 [1024, 1024], replicated, may hold values from -0.1875 to 0.1875
- neigh_list: int32 [128, 3, 6], P('tile'), may hold values from 0 to 8
- neigh_count: int32 [128, 3], P('tile'), may hold values from 1 to 6, as said below
- cross_list: int32 [4, 128, 3, 4], P('frame', 'tile'), may hold values from 0 to 11
Outputs:
- update: bfloat16 [4, 24576, 1024], P('frame', 'tile')
Inputs may be any that keep to these rules, and one draw needn't show every extreme that they name: `neigh_list`: an entry names a block of the extended row of tiles west, own and east, in that order. `neigh_count`: some query block uses all 6 slots. `cross_list`: an entry is frame * 3 + block at the query's own tile.
All inputs are finite; a program needn't handle non-finite values.
Results may differ from a plain program's by a relative error of at most 0.006.
The roundings to bfloat16 on the way count: a program that leaves them out, or rounds other values in their place, can miss the bound.
Values may be sent and summed in bfloat16 or wider, within the bound.
No kernel may reach another device: no remote copies, remote signals or barrier semaphores. Data moves between devices by JAX's collectives and lax.ppermute only.
A program may use at most 128 MiB of HBM per device.

v0:
```python
import jax
import jax.numpy as jnp
from jax import lax
from jax.sharding import PartitionSpec as P

HEADS = 16
NS = 6


def padded(cells, sides, width):
    for axis, dim in sides:
        count = lax.axis_size(axis)
        head = lax.slice_in_dim(cells, 0, width, axis=dim)
        tail = lax.slice_in_dim(cells, cells.shape[dim] - width, cells.shape[dim], axis=dim)
        cells = jnp.concatenate(
            [
                lax.ppermute(tail, axis, [(i, (i + 1) % count) for i in range(count)]),
                cells,
                lax.ppermute(head, axis, [((i + 1) % count, i) for i in range(count)]),
            ],
            axis=dim,
        )
    return cells


def normalize(tokens, norm_gain, modulation):
    values32 = tokens.astype(jnp.float32)
    meansq = jnp.mean(values32 * values32, axis=-1, keepdims=True)
    scaled = values32 * lax.rsqrt(meansq + 1e-06) * norm_gain * (1.0 + modulation[:, None, :])
    return scaled.astype(jnp.bfloat16)


def project(rows, weight):
    return jnp.dot(rows, weight, preferred_element_type=jnp.float32).astype(jnp.bfloat16)


def key_value(blocked, w_key, w_value):
    model_width = blocked.shape[-1]
    flat_rows = blocked.reshape(-1, model_width)
    stacked = jnp.stack([project(flat_rows, w_key), project(flat_rows, w_value)])
    return stacked.reshape((2,) + blocked.shape)


def attend(queries, near_k, near_v, far_k, far_v, near_list, near_count, far_list):
    frames_here, blocks, block_tok, model_width = queries.shape
    ext_blocks = near_k.shape[1]
    head_size = model_width // HEADS
    offset = (jnp.arange(frames_here, dtype=jnp.int32) * ext_blocks)[:, None, None]
    near_index = offset + near_list[None]
    flat_k = near_k.reshape(frames_here * ext_blocks, block_tok, model_width)
    flat_v = near_v.reshape(frames_here * ext_blocks, block_tok, model_width)
    key_set = jnp.concatenate([flat_k[near_index], far_k[far_list]], axis=2)
    value_set = jnp.concatenate([flat_v[near_index], far_v[far_list]], axis=2)
    slot_count = key_set.shape[2]
    key_set = key_set.reshape(frames_here, blocks, slot_count * block_tok, HEADS, head_size)
    value_set = value_set.reshape(frames_here, blocks, slot_count * block_tok, HEADS, head_size)
    usable = jnp.concatenate(
        [
            jnp.arange(NS, dtype=jnp.int32)[None, :] < near_count[:, None],
            jnp.ones((blocks, far_list.shape[-1]), bool),
        ],
        axis=1,
    )
    usable = jnp.repeat(usable, block_tok, axis=1)
    mask_bias = jnp.where(usable, jnp.float32(0.0), jnp.float32(-1e30))
    heads_q = queries.reshape(frames_here, blocks, block_tok, HEADS, head_size)
    scores = jnp.einsum(
        "fbqhd,fbkhd->fbhqk", heads_q, key_set, preferred_element_type=jnp.float32
    ) / jnp.sqrt(jnp.float32(head_size))
    scores = scores + mask_bias[None, :, None, None, :]
    peak_score = jnp.max(scores, axis=-1, keepdims=True)
    shifted = jnp.exp(scores - peak_score)
    weights = (shifted / jnp.sum(shifted, axis=-1, keepdims=True)).astype(jnp.bfloat16)
    attended = jnp.einsum(
        "fbhqk,fbkhd->fbqhd", weights, value_set, preferred_element_type=jnp.float32
    )
    return attended.astype(jnp.bfloat16).reshape(frames_here, blocks, block_tok, model_width)


def local(
    tokens,
    norm_gain,
    modulation,
    w_query,
    w_key,
    w_value,
    w_out,
    neigh_list,
    neigh_count,
    cross_list,
):
    frames_here, tile_tok, model_width = tokens.shape
    blocks = neigh_list.shape[1]
    block_tok = tile_tok // blocks
    normed = normalize(tokens, norm_gain, modulation)
    blocked = normed.reshape(frames_here, blocks, block_tok, model_width)
    queries = project(normed.reshape(-1, model_width), w_query).reshape(blocked.shape)
    own_kv = key_value(blocked, w_key, w_value)
    extended = padded(own_kv, (("tile", 2),), blocks)
    gathered = lax.all_gather(own_kv, "frame", axis=1, tiled=True)
    frames_all = gathered.shape[1]
    far_k = gathered[0].reshape(frames_all * blocks, block_tok, model_width)
    far_v = gathered[1].reshape(frames_all * blocks, block_tok, model_width)
    attended = attend(
        queries,
        extended[0],
        extended[1],
        far_k,
        far_v,
        neigh_list[0],
        neigh_count[0],
        cross_list[:, 0],
    )
    update = jnp.dot(
        attended.reshape(-1, model_width), w_out, preferred_element_type=jnp.float32
    ).astype(jnp.bfloat16)
    return update.reshape(frames_here, tile_tok, model_width)


def solution(mesh):
    return jax.shard_map(
        local,
        mesh=mesh,
        in_specs=(
            P("frame", "tile", None),
            P(),
            P("frame", None),
            P(),
            P(),
            P(),
            P(),
            P("tile", None, None),
            P("tile", None),
            P("frame", "tile", None, None),
        ),
        out_specs=P("frame", "tile", None),
        check_vma=False,
    )
```

profile of v0, /device:TPU:155, one launch (start us, length us, event | category | flops | bytes accessed | tf_op | source)
XLA Modules:
  0.0 235.0 jit_solution(822084720502645016)
XLA Ops:
  6.5 0.0 copy-start
  6.5 0.0 all-gather.2.cloned.1.call-start
  6.5 0.8 broadcast_add_fusion
  7.4 1.4 fusion.12
  8.8 0.0 copy-start.7
  8.8 1.6 fusion.15
  10.4 0.0 copy-start.3
  10.4 0.0 copy-done
  10.4 1.0 convolution_convert_fusion.3
  11.4 0.0 copy-done.7
  11.4 1.0 convolution_convert_fusion.2
  12.4 0.0 copy-done.3
  12.4 0.0 copy-start.6
  12.4 0.0 copy-start.5
  12.4 0.0 copy-start.4
  12.4 1.3 pad_maximum_fusion.3
  13.8 0.0 all-gather.2.cloned.1.call-update
  13.8 2.5 %collective-permute-start = (bf16[2,2,3,64,1024]{4,3,2,1,0:T(8,128)(2,1)}, bf16[2,2,3,64,1024]{4,3,2,1,0:T(8,128)(2,1)}, u32[]{:S(2)}, u32[]{:S(2)}) collective-permute-start(bf16[2,2,3,64,1024]{4,3,2,1,0:T(8,128)(2,1)} %pad_maximum_fusion.3), channel_id=1, source_target_pairs={{0,1},{1,2},{2,3},{3,4},{4,5},{5,6},{6,7},{7,8},{8,9},{9,10},{10,1... | collective-permute-start | bytes 4718600 | tf_op jit(solution)/shard_map/ppermute | solution.py:17
  16.3 0.0 collective-permute-start.1
  16.3 0.0 copy-done.6
  16.3 0.1 compare_select_fusion.1
  16.4 0.1 reshape.87
  16.4 0.0 copy-done.5
  16.5 0.1 reshape.95
  16.5 0.0 copy-done.4
  16.6 0.0 copy-start.8
  16.6 3.5 %convolution_convert_fusion.1 = bf16[384,1024]{1,0:T(8,128)(2,1)} fusion(bf16[384,1024]{1,0:T(8,128)(2,1)S(1)} %bitcast.52, bf16[1024,1024]{1,0:T(8,128)(2,1)} %param.13), kind=kOutput, calls=%fused_computation.30 | convolution fusion | flops 805699584 | bytes 3670016 | tf_op jit(solution)/shard_map/dot_general | solution.py:34
  20.0 3.2 %reshape_reshape.10 = bf16[2,3,64,16,64]{4,3,2,1,0:T(8,128)(2,1)} reshape(bf16[384,1024]{1,0:T(8,128)(2,1)} %convolution_convert_fusion.1) | data formatting | bytes 1572864 | tf_op jit(solution)/shard_map/reshape;reshape | solution.py:66
  23.2 0.0 copy-done.8
  23.2 0.1 iota_compare_fusion
  23.3 0.1 broadcast_in_dim.10
  23.4 0.1 select_n.37
  23.5 43.0 %collective-permute-done = bf16[2,2,3,64,1024]{4,3,2,1,0:T(8,128)(2,1)} collective-permute-done((bf16[2,2,3,64,1024]{4,3,2,1,0:T(8,128)(2,1)}, bf16[2,2,3,64,1024]{4,3,2,1,0:T(8,128)(2,1)}, u32[]{:S(2)}, u32[]{:S(2)}) %collective-permute-start) | collective-permute-done | bytes 1572896 | tf_op jit(solution)/shard_map/ppermute | solution.py:17
  66.4 21.2 %collective-permute-done.1 = bf16[2,2,3,64,1024]{4,3,2,1,0:T(8,128)(2,1)} collective-permute-done((bf16[2,2,3,64,1024]{4,3,2,1,0:T(8,128)(2,1)}, bf16[2,2,3,64,1024]{4,3,2,1,0:T(8,128)(2,1)}, u32[]{:S(2)}, u32[]{:S(2)}) %collective-permute-start.1) | collective-permute-done | bytes 1572896 | tf_op jit(solution)/shard_map/ppermute | solution.py:19
  87.6 2.1 pad_maximum_fusion.2
  89.8 2.6 %fusion.21 = (bf16[1,2,9,64,1024]{4,3,2,1,0:T(8,128)(2,1)}, bf16[1,2,9,64,1024]{4,3,2,1,0:T(8,128)(2,1)}) fusion(bf16[2,2,9,64,1024]{4,3,2,1,0:T(8,128)(2,1)S(1)} %pad_maximum_fusion.2), kind=kLoop, calls=%fused_computation.44 | loop fusion | bytes 9437184 | tf_op jit(solution)/shard_map/slice | solution.py:107
  92.4 6.1 %gather_fusion.2 = bf16[36,64,1024]{2,1,0:T(8,128)(2,1)} fusion(bf16[18,64,1024]{2,1,0:T(8,128)(2,1)} %bitcast.39, s32[1024]{0:T(1024)S(1)} %pad_clamp_fusion.1), kind=kCustom, calls=%fused_computation.2 | custom fusion | bytes 9437328 | tf_op jit(solution)/shard_map/gather | solution.py:52
  98.5 6.2 %gather_fusion = bf16[36,64,1024]{2,1,0:T(8,128)(2,1)} fusion(bf16[18,64,1024]{2,1,0:T(8,128)(2,1)} %bitcast.38, s32[1024]{0:T(1024)S(1)} %pad_clamp_fusion.1), kind=kCustom, calls=%fused_computation | custom fusion | bytes 9437328 | tf_op jit(solution)/shard_map/gather | solution.py:53
  104.7 0.0 all-gather.2.cloned.1.call-done
  104.7 3.6 %fusion.22 = (bf16[1,4,3,64,1024]{4,3,2,1,0:T(8,128)(2,1)S(1)}, bf16[1,4,3,64,1024]{4,3,2,1,0:T(8,128)(2,1)}) fusion(bf16[2,4,3,64,1024]{4,3,2,1,0:T(8,128)(2,1)} %all-gather.2.cloned.1.call-done), kind=kLoop, calls=%fused_computation.45 | loop fusion | bytes 6291456 | tf_op jit(solution)/shard_map/slice | solution.py:103
  108.3 3.9 %gather_fusion.3 = bf16[24,64,1024]{2,1,0:T(8,128)(2,1)} fusion(bf16[12,64,1024]{2,1,0:T(8,128)(2,1)} %bitcast.43, s32[1024]{0:T(1024)S(1)} %pad_clamp_fusion), kind=kCustom, calls=%fused_computation.3 | custom fusion | bytes 6291552 | tf_op jit(solution)/shard_map/gather | solution.py:52
  112.2 7.1 %pad_maximum_fusion.1 = bf16[2,3,10,64,1024]{4,3,2,1,0:T(8,128)(2,1)} fusion(bf16[2,3,4,64,1024]{4,3,2,1,0:T(8,128)(2,1)} %bitcast.45, bf16[2,3,6,64,1024]{4,3,2,1,0:T(8,128)(2,1)} %bitcast.41), kind=kLoop, calls=%fused_computation.14 | loop fusion | flops 3932160 | bytes 15728640 | tf_op jit(solution)/shard_map/concatenate | solution.py:52
  119.3 20.7 %reshape.83 = bf16[2,3,640,16,64]{4,3,2,1,0:T(8,128)(2,1)} reshape(bf16[2,3,10,64,1024]{4,3,2,1,0:T(8,128)(2,1)} %pad_maximum_fusion.1) | data formatting | bytes 15728640 | tf_op jit(solution)/shard_map/reshape | solution.py:55
  140.0 2.6 %gather_fusion.1 = bf16[24,64,1024]{2,1,0:T(8,128)(2,1)} fusion(bf16[12,64,1024]{2,1,0:T(8,128)(2,1)S(1)} %bitcast.42, s32[1024]{0:T(1024)S(1)} %pad_clamp_fusion), kind=kCustom, calls=%fused_computation.1 | custom fusion | bytes 6291552 | tf_op jit(solution)/shard_map/gather | solution.py:53
  142.6 7.1 %pad_maximum_fusion = bf16[2,3,10,64,1024]{4,3,2,1,0:T(8,128)(2,1)} fusion(bf16[2,3,4,64,1024]{4,3,2,1,0:T(8,128)(2,1)} %bitcast.44, bf16[2,3,6,64,1024]{4,3,2,1,0:T(8,128)(2,1)} %bitcast.40), kind=kLoop, calls=%fused_computation.13 | loop fusion | flops 3932160 | bytes 15728640 | tf_op jit(solution)/shard_map/concatenate | solution.py:53
  149.7 0.0 copy-start.2
  149.7 20.8 %reshape.82 = bf16[2,3,640,16,64]{4,3,2,1,0:T(8,128)(2,1)} reshape(bf16[2,3,10,64,1024]{4,3,2,1,0:T(8,128)(2,1)} %pad_maximum_fusion) | data formatting | bytes 15728640 | tf_op jit(solution)/shard_map/reshape | solution.py:56
  170.4 0.0 copy-done.2
  170.4 16.0 %fusion.3 = f32[2,3,16,64,640]{4,3,2,1,0:T(8,128)} fusion(bf16[2,3,640,16,64]{4,3,2,1,0:T(8,128)(2,1)} %reshape.83, bf16[2,3,64,16,64]{4,3,2,1,0:T(8,128)(2,1)S(1)} %copy-done.2), kind=kOutput, calls=%fused_computation.7 | convolution fusion | flops 503316480 | bytes 24379392 | tf_op jit(solution)/shard_map/fbqhd,fbkhd->fbhqk/dot_general | solution.py:67
  186.4 18.0 %fusion.23 = (f32[2,3,16,64]{3,2,1,0:T(8,128)S(1)}, f32[2,3,16,64,640]{4,3,2,1,0:T(8,128)}) fusion(f32[2,3,16,64,640]{4,3,2,1,0:T(8,128)} %fusion.3, f32[3,640]{1,0:T(4,128)S(1)} %select_n.37), kind=kOutput, calls=%fused_computation.46 | output fusion | flops 23593600 | bytes 31489536 | tf_op jit(solution)/shard_map/sub | solution.py:72
  204.5 15.2 %fusion.17 = bf16[2,3,64,16,64]{2,4,3,1,0:T(8,128)(2,1)S(1)} fusion(f32[2,3,16,64,640]{4,3,2,1,0:T(8,128)} %get-tuple-element.10, f32[2,3,16,64]{3,2,1,0:T(8,128)S(1)} %get-tuple-element.9, bf16[2,3,640,16,64]{4,3,2,1,0:T(8,128)(2,1)} %reshape.82), kind=kOutput, calls=%fused_computation.28 | convolution fusion | flops 511574016 | bytes 24403968 | tf_op jit(solution)/shard_map/fbhqk,fbkhd->fbqhd/dot_general | solution.py:74
  219.6 2.2 copy.19
  221.8 0.0 copy-start.1
  221.8 2.8 %reshape_reshape.11 = bf16[384,1024]{1,0:T(8,128)(2,1)S(1)} reshape(bf16[2,3,64,16,64]{4,3,2,1,0:T(8,128)(2,1)} %copy.19) | data formatting | bytes 1572864 | tf_op jit(solution)/shard_map/reshape;reshape | solution.py:115
  224.7 3.5 %convolution_convert_fusion = bf16[384,1024]{1,0:T(8,128)(2,1)} fusion(bf16[384,1024]{1,0:T(8,128)(2,1)S(1)} %reshape_reshape.11, bf16[1024,1024]{1,0:T(8,128)(2,1)} %param.16), kind=kOutput, calls=%fused_computation.29 | convolution fusion | flops 805699584 | bytes 3670016 | tf_op jit(solution)/shard_map/dot_general | solution.py:114
  228.1 0.0 copy-done.1
  (8 shorter events, 0.0 us)
Async XLA Ops:
  6.5 3.8 %copy-start = (bf16[1024,1024]{1,0:T(8,128)(2,1)S(1)}, bf16[1024,1024]{1,0:T(8,128)(2,1)}, u32[]{:S(2)}) copy-start(bf16[1024,1024]{1,0:T(8,128)(2,1)} %param.14) | copy-start | bytes 6291460
  6.5 98.2 %all-gather.2.cloned.1.call-start = ((), (), s32[]{:S(2)}) async-start(), calls=%async_computation | async-start | bytes 4718592 | tf_op jit(solution)/shard_map/all_gather | solution.py:100
  8.8 2.6 %copy-start.7 = (bf16[1024,1024]{1,0:T(8,128)(2,1)S(1)}, bf16[1024,1024]{1,0:T(8,128)(2,1)}, u32[]{:S(2)}) copy-start(bf16[1024,1024]{1,0:T(8,128)(2,1)} %param.15) | copy-start | bytes 6291460
  10.4 2.0 copy-start.3
  12.4 3.9 %copy-start.6 = (s32[1,3,6]{2,0,1:T(1,128)S(1)}, s32[1,3,6]{2,0,1:T(1,128)}, u32[]{:S(2)}) copy-start(s32[1,3,6]{2,0,1:T(1,128)} %param.17) | copy-start | bytes 220
  12.4 4.0 %copy-start.5 = (s32[2,1,3,4]{3,1,2,0:T(1,128)S(1)}, s32[2,1,3,4]{3,1,2,0:T(1,128)}, u32[]{:S(2)}) copy-start(s32[2,1,3,4]{3,1,2,0:T(1,128)} %param.19) | copy-start | bytes 292
  12.4 4.1 %copy-start.4 = (bf16[2,192,1024]{2,1,0:T(8,128)(2,1)S(1)}, bf16[2,192,1024]{2,1,0:T(8,128)(2,1)}, u32[]{:S(2)}) copy-start(bf16[2,192,1024]{2,1,0:T(8,128)(2,1)} %copy-done.3) | copy-start | bytes 2359300
  13.8 52.7 %collective-permute-start = (bf16[2,2,3,64,1024]{4,3,2,1,0:T(8,128)(2,1)}, bf16[2,2,3,64,1024]{4,3,2,1,0:T(8,128)(2,1)}, u32[]{:S(2)}, u32[]{:S(2)}) collective-permute-start(bf16[2,2,3,64,1024]{4,3,2,1,0:T(8,128)(2,1)} %pad_maximum_fusion.3), channel_id=1, source_target_pairs={{0,1},{1,2},{2,3},{3,4},{4,5},{5,6},{6,7},{7,8},{8,9},{9,10},{10,1... | collective-permute-start | bytes 4718600 | tf_op jit(solution)/shard_map/ppermute | solution.py:17
  16.3 71.4 %collective-permute-start.1 = (bf16[2,2,3,64,1024]{4,3,2,1,0:T(8,128)(2,1)}, bf16[2,2,3,64,1024]{4,3,2,1,0:T(8,128)(2,1)}, u32[]{:S(2)}, u32[]{:S(2)}) collective-permute-start(bf16[2,2,3,64,1024]{4,3,2,1,0:T(8,128)(2,1)} %pad_maximum_fusion.3), channel_id=1, source_target_pairs={{1,0},{2,1},{3,2},{4,3},{5,4},{6,5},{7,6},{8,7},{9,8},{10,9},{11,1... | collective-permute-start | bytes 4718600 | tf_op jit(solution)/shard_map/ppermute | solution.py:19
  16.6 6.7 %copy-start.8 = (s32[1,3]{1,0:T(1,128)S(1)}, s32[1,3]{1,0:T(1,128)}, u32[]{:S(2)}) copy-start(s32[1,3]{1,0:T(1,128)} %param.18) | copy-start | bytes 40
  149.7 20.8 %copy-start.2 = (bf16[2,3,64,16,64]{4,3,2,1,0:T(8,128)(2,1)S(1)}, bf16[2,3,64,16,64]{4,3,2,1,0:T(8,128)(2,1)}, u32[]{:S(2)}) copy-start(bf16[2,3,64,16,64]{4,3,2,1,0:T(8,128)(2,1)} %reshape_reshape.10) | copy-start | bytes 2359300
  221.8 6.3 %copy-start.1 = (bf16[1024,1024]{1,0:T(8,128)(2,1)S(1)}, bf16[1024,1024]{1,0:T(8,128)(2,1)}, u32[]{:S(2)}) copy-start(bf16[1024,1024]{1,0:T(8,128)(2,1)} %param.14) | copy-start | bytes 6291460
Sparse Core Ops, SparseCore 0:
  13.9 72.5 all-gather.1
where the time goes:
time: 236 us; the launch traced here: 235 us
  local copies, waits for them, and re-layouts  75.1 us (32%)
  waiting for transfers between devices  64.2 us (27%)
  matrix products  40.1 us (17%)
  other arithmetic  39.6 us (17%)
  between operations  13.6 us (6%)
  starting transfers between devices  2.49 us (1%)
    ppermute x1, waiting for transfers between devices, padded(): lax.ppermute(tail, axis, [(i, (i + 1) % count) for i in range(count)])  43 us
    ppermute x1, waiting for transfers between devices, padded(): lax.ppermute(head, axis, [((i + 1) % count, i) for i in range(count)])  21.2 us
    reshape x1, local copies, waits for them, and re-layouts, attend(): value_set.reshape(frames_here, blocks, slot_count * block_tok, HEADS, hea...  20.8 us
    reshape x1, local copies, waits for them, and re-layouts, attend(): key_set.reshape(frames_here, blocks, slot_count * block_tok, HEADS, head_...  20.7 us
    sub x1, other arithmetic, attend(): shifted = jnp.exp(scores - peak_score)  18 us
    dot_general x1, matrix products, attend(): jnp.einsum('fbqhd,fbkhd->fbhqk', heads_q, key_set, preferred_element_type...  16 us
    dot_general x1, matrix products, attend(): jnp.einsum('fbhqk,fbkhd->fbqhd', weights, value_set, preferred_element_ty...  15.2 us
    gather x2, local copies, waits for them, and re-layouts, attend(): key_set = jnp.concatenate([flat_k[near_index], far_k[far_list]], axis=2)  10 us
  transfers between devices with their start and end apart: 3, of which 2 were waited for; matrix products, arithmetic and copies ran while one was open for 10% of the time, Pallas kernels for 0%

commit v1 on v0

v1 whole, which is shorter than its diff:
```python
import functools

import jax
import jax.numpy as jnp
import numpy as np
from jax import lax
from jax.experimental import pallas as pl
from jax.experimental.pallas import tpu as pltpu
from jax.sharding import PartitionSpec as P

HEADS = 16
NS = 6
CS = 4
SLOTS = NS + CS
BT = 64
NBLK = 3
D = 1024
HEAD = D // HEADS
GROUP = 4
GW = GROUP * HEAD
TOK = NBLK * BT
ROWS = 2 * TOK
CHUNKS = 4
CR = ROWS // CHUNKS
BOTH = ("frame", "tile")
VMEM = pl.BlockSpec(memory_space=pltpu.VMEM)
SMEM = pl.BlockSpec(memory_space=pltpu.SMEM)
ANY = pl.BlockSpec(memory_space=pl.ANY)
EXP_SCALE = float(np.log2(np.e) / np.sqrt(HEAD))


def params(limit):
    return pltpu.CompilerParams(vmem_limit_bytes=limit)


def cost(flops, nbytes):
    return pl.CostEstimate(flops=int(flops), bytes_accessed=int(nbytes), transcendentals=0)


def norm_kernel(tok_ref, gain_ref, mod_ref, whole_ref, *chunk_refs):
    for i in range(CHUNKS):
        frame, row = divmod(i * CR, TOK)
        x = tok_ref[frame, row : row + CR, :].astype(jnp.float32)
        meansq = jnp.mean(x * x, axis=-1, keepdims=True)
        scaled = x * lax.rsqrt(meansq + 1e-06) * gain_ref[...] * (1.0 + mod_ref[frame : frame + 1, :])
        normed = scaled.astype(jnp.bfloat16)
        whole_ref[i * CR : (i + 1) * CR, :] = normed
        chunk_refs[i][...] = normed


def norm(tokens, gain, mod):
    chunk = jax.ShapeDtypeStruct((CR, D), jnp.bfloat16)
    return pl.pallas_call(
        norm_kernel,
        out_shape=[jax.ShapeDtypeStruct((ROWS, D), jnp.bfloat16)] + [chunk] * CHUNKS,
        in_specs=[VMEM] * 3,
        out_specs=[VMEM] * (1 + CHUNKS),
        compiler_params=params(8 << 20),
        cost_estimate=cost(ROWS * D * 8, ROWS * D * 6),
    )(tokens, gain, mod)


def project_into(x_ref, w_ref, out_ref, at):
    rows = x_ref.shape[0]
    for c in range(0, D, 256):
        out_ref[at : at + rows, c : c + 256] = jnp.dot(
            x_ref[...], w_ref[:, c : c + 256], preferred_element_type=jnp.float32
        ).astype(jnp.bfloat16)


def own_kernel(x_ref, wq_ref, wk_ref, wv_ref, q_ref, k_ref, v_ref):
    project_into(x_ref, wq_ref, q_ref, 0)
    project_into(x_ref, wk_ref, k_ref, 0)
    project_into(x_ref, wv_ref, v_ref, 0)


def own_project(x, wq, wk, wv):
    held = jax.ShapeDtypeStruct((4 * ROWS, D), jnp.bfloat16)
    return pl.pallas_call(
        own_kernel,
        out_shape=[jax.ShapeDtypeStruct((ROWS, D), jnp.bfloat16), held, held],
        in_specs=[VMEM] * 4,
        out_specs=[VMEM] * 3,
        compiler_params=params(8 << 20),
        cost_estimate=cost(6 * ROWS * D * D, 8 * D * D),
    )(x, wq, wk, wv)


def kv_kernel(ats, *refs):
    n = len(ats)
    wk_ref, wv_ref, _, _, k_ref, v_ref = refs[n:]
    for x_ref, at in zip(refs[:n], ats):
        project_into(x_ref, wk_ref, k_ref, at)
        project_into(x_ref, wv_ref, v_ref, at)


def kv_project(xs, ats, wk, wv, keys, values):
    n = len(xs)
    rows = sum(x.shape[0] for x in xs)
    held = jax.ShapeDtypeStruct((4 * ROWS, D), jnp.bfloat16)
    return pl.pallas_call(
        functools.partial(kv_kernel, ats),
        out_shape=[held, held],
        in_specs=[VMEM] * (n + 4),
        out_specs=[VMEM] * 2,
        input_output_aliases={n + 2: 0, n + 3: 1},
        compiler_params=params(8 << 20),
        cost_estimate=cost(4 * rows * D * D, 6 * D * D),
    )(*xs, wk, wv, keys, values)


def attend_kernel(frame, slot_ref, count_ref, q_ref, k_ref, v_ref, wo_ref, *rest):
    out_ref, att_ref, upd_ref, sem = rest[-4:]
    r = lax.broadcasted_iota(jnp.int32, (GW, GW), 0) // HEAD
    c = lax.broadcasted_iota(jnp.int32, (GW, GW), 1) // HEAD
    diagonal = r == c
    lane = lax.broadcasted_iota(jnp.int32, (1, SLOTS * BT), 1) // BT

    def block(b, g):
        u = frame * NBLK + b
        cols = slice(g * GW, (g + 1) * GW)
        q = q_ref[u * BT : (u + 1) * BT, cols]
        q4 = jnp.concatenate([q] * GROUP, axis=0)
        q4 = jnp.where(diagonal, q4, jnp.zeros_like(q4))
        at = [pl.ds(pl.multiple_of(slot_ref[u * SLOTS + s] * BT, BT), BT) for s in range(SLOTS)]
        keys = jnp.concatenate([k_ref[a, cols] for a in at], axis=0)
        values = jnp.concatenate([v_ref[a, cols] for a in at], axis=0)
        scores = lax.dot_general(
            q4, keys, (((1,), (1,)), ((), ())), preferred_element_type=jnp.float32
        )
        unused = (lane >= count_ref[b]) & (lane < NS)
        scores = scores + jnp.where(unused, jnp.float32(-1e30), jnp.float32(0.0))
        peak = jnp.max(scores, axis=1, keepdims=True)
        weights = jnp.exp2((scores - peak) * EXP_SCALE)
        total = jnp.sum(weights, axis=1, keepdims=True)
        att = jnp.dot(weights.astype(jnp.bfloat16), values, preferred_element_type=jnp.float32)
        att = jnp.where(diagonal, att * (1.0 / total), 0.0)
        att = sum(att[h * BT : (h + 1) * BT] for h in range(GROUP))
        att_ref[b * BT : (b + 1) * BT, cols] = att.astype(jnp.bfloat16)

    for g in range(D // GW):
        for b in range(NBLK):
            block(b, g)
    copies = []
    for i, col in enumerate(range(0, D, 256)):
        upd_ref[:, col : col + 256] = jnp.dot(
            att_ref[...], wo_ref[:, col : col + 256], preferred_element_type=jnp.float32
        ).astype(jnp.bfloat16)
    copy = pltpu.make_async_copy(upd_ref, out_ref.at[frame], sem)
    copy.start()
    copy.wait()


def attend(frame, slots, counts, queries, keys, values, w_out, earlier=None):
    extra = [] if earlier is None else [earlier]
    return pl.pallas_call(
        functools.partial(attend_kernel, frame),
        out_shape=jax.ShapeDtypeStruct((2, TOK, D), jnp.bfloat16),
        in_specs=[SMEM] * 2 + [VMEM] * 4 + [ANY] * len(extra),
        out_specs=ANY,
        scratch_shapes=[
            pltpu.VMEM((TOK, D), jnp.bfloat16),
            pltpu.VMEM((TOK, D), jnp.bfloat16),
            pltpu.SemaphoreType.DMA,
        ],
        input_output_aliases={6: 0} if extra else {},
        compiler_params=params(16 << 20),
        cost_estimate=cost(2 * TOK * D * D + 16 * TOK * SLOTS * BT * D, 8 * D * D),
    )(slots, counts, queries, keys, values, w_out, *extra)


def slot_table(neigh, cross, parity, mine):
    side = neigh // NBLK
    source = jnp.where(side == 1, 0, jnp.where((side == 2) == (parity == 0), 2, 3))
    near = source * 2 * NBLK + neigh % NBLK
    near = near[None] + NBLK * jnp.arange(2, dtype=jnp.int32)[:, None, None]
    owner = cross // (2 * NBLK)
    far = jnp.where(owner == mine, 0, 2 * NBLK) + cross % (2 * NBLK)
    return jnp.concatenate([near, far], axis=-1).reshape(-1)


def local(tokens, norm_gain, modulation, w_query, w_key, w_value, w_out, neigh_list, neigh_count, cross_list):
    tiles = lax.axis_size("tile")
    mine = lax.axis_index("frame")
    tile = lax.axis_index("tile")

    def device(f, t):
        return f * tiles + t % tiles

    cells = [(f, t) for f in range(2) for t in range(tiles)]
    partner = [(device(f, t), device(1 - f, t)) for f, t in cells]
    pair = [(device(f, t), device(f, t ^ 1)) for f, t in cells]
    onward = [(device(f, t), device(1 - f, t + 1 if t % 2 else t - 1)) for f, t in cells]

    slots = slot_table(neigh_list[0], cross_list[:, 0], tile % 2, mine)
    whole, *chunks = norm(tokens, norm_gain[None], modulation)
    swapped = [lax.ppermute(c, BOTH, partner) for c in chunks]
    across = lax.ppermute(whole, BOTH, pair)
    beyond = [lax.ppermute(s, BOTH, onward) for s in swapped]

    queries, keys, values = own_project(whole, w_query, w_key, w_value)
    keys, values = kv_project([across], [2 * ROWS], w_key, w_value, keys, values)
    for i in range(CHUNKS):
        keys, values = kv_project([swapped[i]], [ROWS + i * CR], w_key, w_value, keys, values)
        if i:
            keys, values = kv_project([beyond[i - 1]], [3 * ROWS + (i - 1) * CR], w_key, w_value, keys, values)
    last = CHUNKS - 1
    first = attend(0, slots, neigh_count[0], queries, keys, values, w_out)
    keys, values = kv_project([beyond[last]], [3 * ROWS + last * CR], w_key, w_value, keys, values)
    return attend(1, slots, neigh_count[0], queries, keys, values, w_out, first)


def solution(mesh):
    return jax.shard_map(
        local,
        mesh=mesh,
        in_specs=(
            P("frame", "tile", None),
            P(),
            P("frame", None),
            P(),
            P(),
            P(),
            P(),
            P("tile", None, None),
            P("tile", None),
            P("frame", "tile", None, None),
        ),
        out_specs=P("frame", "tile", None),
        check_vma=False,
    )
```

time: 236 us -> 52.5 us (0.22)
  the two profiles are of different devices: /device:TPU:155 before, /device:TPU:0 now
where the time goes in v1:
time: 52.5 us; the launch traced here: 52.1 us
  Pallas kernels  21.9 us (42%)
  starting transfers between devices  19.4 us (37%)
  local copies, waits for them, and re-layouts  8.17 us (16%)
  other arithmetic  2.26 us (4%)
    ppermute x4, starting transfers between devices, local(): beyond = [lax.ppermute(s, BOTH, onward) for s in swapped]  15.2 us
    pallas_call x2, Pallas kernels, attend(): pl.pallas_call(functools.partial(attend_kernel, frame), out_shape=jax.Sha...  10.7 us
    pallas_call x9, Pallas kernels, kv_project(): pl.pallas_call(functools.partial(kv_kernel, ats), out_shape=[held, held],...  8.2 us
    unnamed x21, local copies, waits for them, and re-layouts  8.08 us
    ppermute x4, starting transfers between devices, local(): swapped = [lax.ppermute(c, BOTH, partner) for c in chunks]  4.13 us
    pallas_call x1, Pallas kernels, own_project(): pl.pallas_call(own_kernel, out_shape=[jax.ShapeDtypeStruct((ROWS, D), jnp...  2.65 us
  transfers between devices with their start and end apart: 9, of which 0 were waited for; matrix products, arithmetic and copies ran while one was open for 5% of the time, Pallas kernels for 30%

profile of v1, /device:TPU:0, one launch (start us, length us, event | category | flops | bytes accessed | tf_op | source)
XLA Modules:
  0.0 52.1 jit_solution(8422860319620421734)
XLA Ops:
  0.0 0.0 copy-start.5
  0.0 1.1 %copy-done.5 = bf16[2,192,1024]{2,1,0:T(8,128)(2,1)S(1)} copy-done((bf16[2,192,1024]{2,1,0:T(8,128)(2,1)S(1)}, bf16[2,192,1024]{2,1,0:T(8,128)(2,1)}, u32[]{:S(2)}) %copy-start.5) | copy-done | bytes 786456
  1.1 0.0 copy-start.6
  1.1 0.7 %copy-done.6 = f32[2,1024]{1,0:T(2,128)S(1)} copy-done((f32[2,1024]{1,0:T(2,128)S(1)}, f32[2,1024]{1,0:T(2,128)}, u32[]{:S(2)}) %copy-start.6) | copy-done | bytes 8216
  1.8 0.0 copy-start.7
  1.8 0.7 %copy-done.7 = f32[1024]{0:T(1024)S(1)} copy-done((f32[1024]{0:T(1024)S(1)}, f32[1024]{0:T(1024)}, u32[]{:S(2)}) %copy-start.7) | copy-done | bytes 4120
  2.5 0.4 shard_map.100
  2.9 0.1 collective-permute-start.8
  3.0 0.1 collective-permute-start.6
  3.1 2.0 %collective-permute-start.4 = (bf16[96,1024]{1,0:T(8,128)(2,1)S(1)}, bf16[96,1024]{1,0:T(8,128)(2,1)S(1)}, u32[]{:S(2)}, u32[]{:S(2)}) collective-permute-start(bf16[96,1024]{1,0:T(8,128)(2,1)S(1)} %get-tuple-element.35), channel_id=1, source_target_pairs={{0,128},{1,129},{2,130},{3,131},{4,132},{5,133},{6,134},{7,135},{8... | collective-permute-start | bytes 589832 | tf_op jit(solution)/shard_map/ppermute | solution.py:197
  5.1 0.1 collective-permute-start.2
  5.2 1.9 %collective-permute-start = (bf16[96,1024]{1,0:T(8,128)(2,1)S(1)}, bf16[96,1024]{1,0:T(8,128)(2,1)S(1)}, u32[]{:S(2)}, u32[]{:S(2)}) collective-permute-start(bf16[96,1024]{1,0:T(8,128)(2,1)S(1)} %get-tuple-element.33), channel_id=1, source_target_pairs={{0,128},{1,129},{2,130},{3,131},{4,132},{5,133},{6,134},{7,135},{8... | collective-permute-start | bytes 589832 | tf_op jit(solution)/shard_map/ppermute | solution.py:197
  7.1 0.7 %fusion.3 = s32[1,3,6]{2,0,1:T(1,128)S(1)} fusion(pred[]{:T(512)S(6)} %eq.32, s32[1,3,6]{2,0,1:T(1,128)} %param.17), kind=kLoop, calls=%fused_computation.18 | loop fusion | flops 342 | bytes 145 | tf_op jit(solution)/shard_map/add | solution.py:175
  7.8 0.7 %broadcast_divide_fusion = (s32[2,1,3,4]{3,1,2,0:T(1,128)S(1)}, s32[2,1,3,4]{3,1,2,0:T(1,128)S(1)}) fusion(s32[2,1,3,4]{3,1,2,0:T(1,128)} %param.19), kind=kLoop, calls=%fused_computation.19 | loop fusion | flops 48 | bytes 288 | tf_op jit(solution)/shard_map/jit(floor_divide)/div | solution.py:177
  8.6 0.1 broadcast_add_fusion
  8.6 0.7 %sign_compare_fusion = pred[2,1,3,4]{3,1,2,0:T(4,128)(4,1)S(1)} fusion(s32[2,1,3,4]{3,1,2,0:T(1,128)} %param.19), kind=kLoop, calls=%fused_computation.15 | loop fusion | flops 48 | bytes 120 | tf_op jit(solution)/shard_map/jit(floor_divide)/ne | solution.py:177
  9.3 0.1 pad_add_fusion
  9.4 0.1 reshape.15.slot_ref
  9.5 0.0 copy-start
  9.5 1.6 %copy-done = bf16[1024,1024]{1,0:T(8,128)(2,1)S(1)} copy-done((bf16[1024,1024]{1,0:T(8,128)(2,1)S(1)}, bf16[1024,1024]{1,0:T(8,128)(2,1)}, u32[]{:S(2)}) %copy-start) | copy-done | bytes 2097176
  11.1 0.0 copy-start.2
  11.1 1.6 %copy-done.2 = bf16[1024,1024]{1,0:T(8,128)(2,1)S(1)} copy-done((bf16[1024,1024]{1,0:T(8,128)(2,1)S(1)}, bf16[1024,1024]{1,0:T(8,128)(2,1)}, u32[]{:S(2)}) %copy-start.2) | copy-done | bytes 2097176
  12.7 0.0 copy-start.9
  12.7 1.6 %copy-done.9 = bf16[1024,1024]{1,0:T(8,128)(2,1)S(1)} copy-done((bf16[1024,1024]{1,0:T(8,128)(2,1)S(1)}, bf16[1024,1024]{1,0:T(8,128)(2,1)}, u32[]{:S(2)}) %copy-start.9) | copy-done | bytes 2097176
  14.3 0.0 copy-start.1
  14.3 2.6 %shard_map.101 = (bf16[384,1024]{1,0:T(8,128)(2,1)S(1)}, bf16[1536,1024]{1,0:T(8,128)(2,1)S(1)}, bf16[1536,1024]{1,0:T(8,128)(2,1)S(1)}) custom-call(bf16[384,1024]{1,0:T(8,128)(2,1)S(1)} %get-tuple-element.31.x_ref, bf16[1024,1024]{1,0:T(8,128)(2,1)S(1)} %copy-done.9, bf16[1024,1024]{1,0:T(8,128)(2,1)S(1)} %copy-done, bf16[1024,1024]{1,0:T(8,128)(2,1)S(1)} %copy-done.2), custom_call_target="tpu_custom_call" | custom-call | flops 2415919104 | bytes 8388608 | tf_op jit(solution)/shard_map/pallas_call | solution.py:79
  16.9 0.0 collective-permute-done.6.refs_0_
  17.0 7.8 %collective-permute-start.7 = (bf16[96,1024]{1,0:T(8,128)(2,1)S(1)}, bf16[96,1024]{1,0:T(8,128)(2,1)S(1)}, u32[]{:S(2)}, u32[]{:S(2)}) collective-permute-start(bf16[96,1024]{1,0:T(8,128)(2,1)S(1)} %collective-permute-done.6.refs_0_), channel_id=1, source_target_pairs={{0,255},{1,130},{2,129},{3,132},{4,131},{5,134},{6,133},{7,136},{8... | collective-permute-start | bytes 589832 | tf_op jit(solution)/shard_map/ppermute | solution.py:199
  24.7 0.0 collective-permute-done.4.refs_0_
  24.7 0.1 collective-permute-start.5
  24.8 0.0 collective-permute-done.2.refs_0_
  24.8 7.1 %collective-permute-start.3 = (bf16[96,1024]{1,0:T(8,128)(2,1)S(1)}, bf16[96,1024]{1,0:T(8,128)(2,1)S(1)}, u32[]{:S(2)}, u32[]{:S(2)}) collective-permute-start(bf16[96,1024]{1,0:T(8,128)(2,1)S(1)} %collective-permute-done.2.refs_0_), channel_id=1, source_target_pairs={{0,255},{1,130},{2,129},{3,132},{4,131},{5,134},{6,133},{7,136},{8... | collective-permute-start | bytes 589832 | tf_op jit(solution)/shard_map/ppermute | solution.py:199
  31.9 0.0 collective-permute-done.refs_0_
  31.9 0.3 collective-permute-start.1
  32.2 0.0 collective-permute-done.8.refs_0_
  32.2 0.0 copy-done.1
  32.2 1.8 %shard_map.102 = (bf16[1536,1024]{1,0:T(8,128)(2,1)S(1)}, bf16[1536,1024]{1,0:T(8,128)(2,1)S(1)}) custom-call(bf16[384,1024]{1,0:T(8,128)(2,1)S(1)} %collective-permute-done.8.refs_0_, bf16[1024,1024]{1,0:T(8,128)(2,1)S(1)} %copy-done.1, bf16[1024,1024]{1,0:T(8,128)(2,1)S(1)} %copy-done.2, ...), custom_call_target="tpu_custom_call", output_to_operand_aliasing={{0}: (3, {}), {1}: (4, {})} | custom-call | flops 1610612736 | bytes 6291456 | tf_op jit(solution)/shard_map/pallas_call | solution.py:101
  34.0 0.8 %shard_map.103 = (bf16[1536,1024]{1,0:T(8,128)(2,1)S(1)}, bf16[1536,1024]{1,0:T(8,128)(2,1)S(1)}) custom-call(bf16[96,1024]{1,0:T(8,128)(2,1)S(1)} %collective-permute-done.6.refs_0_, bf16[1024,1024]{1,0:T(8,128)(2,1)S(1)} %copy-done.1, bf16[1024,1024]{1,0:T(8,128)(2,1)S(1)} %copy-done.2, ...), custom_call_target="tpu_custom_call", output_to_operand_aliasing={{0}: (3, {}), {1}: (4, {})} | custom-call | flops 402653184 | bytes 6291456 | tf_op jit(solution)/shard_map/pallas_call | solution.py:101
  34.8 0.8 %shard_map.104 = (bf16[1536,1024]{1,0:T(8,128)(2,1)S(1)}, bf16[1536,1024]{1,0:T(8,128)(2,1)S(1)}) custom-call(bf16[96,1024]{1,0:T(8,128)(2,1)S(1)} %collective-permute-done.4.refs_0_, bf16[1024,1024]{1,0:T(8,128)(2,1)S(1)} %copy-done.1, bf16[1024,1024]{1,0:T(8,128)(2,1)S(1)} %copy-done.2, ...), custom_call_target="tpu_custom_call", output_to_operand_aliasing={{0}: (3, {}), {1}: (4, {})} | custom-call | flops 402653184 | bytes 6291456 | tf_op jit(solution)/shard_map/pallas_call | solution.py:101
  35.6 0.0 collective-permute-done.7.refs_0_
  35.6 0.8 %shard_map.105 = (bf16[1536,1024]{1,0:T(8,128)(2,1)S(1)}, bf16[1536,1024]{1,0:T(8,128)(2,1)S(1)}) custom-call(bf16[96,1024]{1,0:T(8,128)(2,1)S(1)} %collective-permute-done.7.refs_0_, bf16[1024,1024]{1,0:T(8,128)(2,1)S(1)} %copy-done.1, bf16[1024,1024]{1,0:T(8,128)(2,1)S(1)} %copy-done.2, ...), custom_call_target="tpu_custom_call", output_to_operand_aliasing={{0}: (3, {}), {1}: (4, {})} | custom-call | flops 402653184 | bytes 6291456 | tf_op jit(solution)/shard_map/pallas_call | solution.py:101
  36.4 0.8 %shard_map.106 = (bf16[1536,1024]{1,0:T(8,128)(2,1)S(1)}, bf16[1536,1024]{1,0:T(8,128)(2,1)S(1)}) custom-call(bf16[96,1024]{1,0:T(8,128)(2,1)S(1)} %collective-permute-done.2.refs_0_, bf16[1024,1024]{1,0:T(8,128)(2,1)S(1)} %copy-done.1, bf16[1024,1024]{1,0:T(8,128)(2,1)S(1)} %copy-done.2, ...), custom_call_target="tpu_custom_call", output_to_operand_aliasing={{0}: (3, {}), {1}: (4, {})} | custom-call | flops 402653184 | bytes 6291456 | tf_op jit(solution)/shard_map/pallas_call | solution.py:101
  37.2 0.0 collective-permute-done.5.refs_0_
  37.2 0.8 %shard_map.107 = (bf16[1536,1024]{1,0:T(8,128)(2,1)S(1)}, bf16[1536,1024]{1,0:T(8,128)(2,1)S(1)}) custom-call(bf16[96,1024]{1,0:T(8,128)(2,1)S(1)} %collective-permute-done.5.refs_0_, bf16[1024,1024]{1,0:T(8,128)(2,1)S(1)} %copy-done.1, bf16[1024,1024]{1,0:T(8,128)(2,1)S(1)} %copy-done.2, ...), custom_call_target="tpu_custom_call", output_to_operand_aliasing={{0}: (3, {}), {1}: (4, {})} | custom-call | flops 402653184 | bytes 6291456 | tf_op jit(solution)/shard_map/pallas_call | solution.py:101
  38.0 0.8 %shard_map.108 = (bf16[1536,1024]{1,0:T(8,128)(2,1)S(1)}, bf16[1536,1024]{1,0:T(8,128)(2,1)S(1)}) custom-call(bf16[96,1024]{1,0:T(8,128)(2,1)S(1)} %collective-permute-done.refs_0_, bf16[1024,1024]{1,0:T(8,128)(2,1)S(1)} %copy-done.1, bf16[1024,1024]{1,0:T(8,128)(2,1)S(1)} %copy-done.2, ...), custom_call_target="tpu_custom_call", output_to_operand_aliasing={{0}: (3, {}), {1}: (4, {})} | custom-call | flops 402653184 | bytes 6291456 | tf_op jit(solution)/shard_map/pallas_call | solution.py:101
  38.8 0.0 collective-permute-done.3.refs_0_
  38.9 0.0 copy-start.4
  38.9 0.0 copy-start.8
  38.9 0.8 %shard_map.109 = (bf16[1536,1024]{1,0:T(8,128)(2,1)S(1)}, bf16[1536,1024]{1,0:T(8,128)(2,1)S(1)}) custom-call(bf16[96,1024]{1,0:T(8,128)(2,1)S(1)} %collective-permute-done.3.refs_0_, bf16[1024,1024]{1,0:T(8,128)(2,1)S(1)} %copy-done.1, bf16[1024,1024]{1,0:T(8,128)(2,1)S(1)} %copy-done.2, ...), custom_call_target="tpu_custom_call", output_to_operand_aliasing={{0}: (3, {}), {1}: (4, {})} | custom-call | flops 402653184 | bytes 6291456 | tf_op jit(solution)/shard_map/pallas_call | solution.py:101
  39.7 0.8 %copy-done.4 = bf16[1024,1024]{1,0:T(8,128)(2,1)S(1)} copy-done((bf16[1024,1024]{1,0:T(8,128)(2,1)S(1)}, bf16[1024,1024]{1,0:T(8,128)(2,1)}, u32[]{:S(2)}) %copy-start.4) | copy-done | bytes 2097176
  40.4 0.0 copy-done.8
  40.5 0.0 copy-start.3
  40.5 5.3 %shard_map.111.rest_0_ = bf16[2,192,1024]{2,1,0:T(8,128)(2,1)} custom-call(s32[60]{0:T(128)S(1)} %reshape.15.slot_ref, s32[3]{0:T(128)S(1)} %bitcast.14, bf16[384,1024]{1,0:T(8,128)(2,1)S(1)} %get-tuple-element.32.q_ref, bf16[1536,1024]{1,0:T(8,128)(2,1)S(1)} %get-tuple-element.53.refs_3_.k_ref, bf16[1536,1024]{1,0:T(8,128)(2,1)S(1)} %get-tuple-element.54.refs_4_.v_ref, ...), custom_call_target="tpu_custom_call" | custom-call | flops 2415919104 | bytes 8388608 | tf_op jit(solution)/shard_map/pallas_call | solution.py:156
  45.8 0.0 collective-permute-done.1.refs_0_
  45.8 0.0 copy-done.3
  45.8 0.8 %shard_map.110 = (bf16[1536,1024]{1,0:T(8,128)(2,1)S(1)}, bf16[1536,1024]{1,0:T(8,128)(2,1)S(1)}) custom-call(bf16[96,1024]{1,0:T(8,128)(2,1)S(1)} %collective-permute-done.1.refs_0_, bf16[1024,1024]{1,0:T(8,128)(2,1)S(1)} %copy-done.1, bf16[1024,1024]{1,0:T(8,128)(2,1)S(1)} %copy-done.3, ...), custom_call_target="tpu_custom_call", output_to_operand_aliasing={{0}: (3, {}), {1}: (4, {})} | custom-call | flops 402653184 | bytes 6291456 | tf_op jit(solution)/shard_map/pallas_call | solution.py:101
  46.6 5.3 %shard_map.112 = bf16[2,192,1024]{2,1,0:T(8,128)(2,1)} custom-call(s32[60]{0:T(128)S(1)} %reshape.15.slot_ref, s32[3]{0:T(128)S(1)} %bitcast.15, bf16[384,1024]{1,0:T(8,128)(2,1)S(1)} %get-tuple-element.32.q_ref, bf16[1536,1024]{1,0:T(8,128)(2,1)S(1)} %get-tuple-element.55.k_ref, ...), custom_call_target="tpu_custom_call", output_to_operand_aliasing={{}: (6, {})} | custom-call | flops 2415919104 | bytes 8388608 | tf_op jit(solution)/shard_map/pallas_call | solution.py:156
  (4 shorter events, 0.0 us)
Async XLA Ops:
  0.0 1.1 %copy-start.5 = (bf16[2,192,1024]{2,1,0:T(8,128)(2,1)S(1)}, bf16[2,192,1024]{2,1,0:T(8,128)(2,1)}, u32[]{:S(2)}) copy-start(bf16[2,192,1024]{2,1,0:T(8,128)(2,1)} %tok_ref.1) | copy-start | bytes 2359300
  1.1 0.7 %copy-start.6 = (f32[2,1024]{1,0:T(2,128)S(1)}, f32[2,1024]{1,0:T(2,128)}, u32[]{:S(2)}) copy-start(f32[2,1024]{1,0:T(2,128)} %mod_ref.1) | copy-start | bytes 24580
  1.8 0.7 %copy-start.7 = (f32[1024]{0:T(1024)S(1)}, f32[1024]{0:T(1024)}, u32[]{:S(2)}) copy-start(f32[1024]{0:T(1024)} %param.11) | copy-start | bytes 12292
  2.9 29.3 %collective-permute-start.8 = (bf16[384,1024]{1,0:T(8,128)(2,1)S(1)}, bf16[384,1024]{1,0:T(8,128)(2,1)S(1)}, u32[]{:S(2)}, u32[]{:S(2)}) collective-permute-start(bf16[384,1024]{1,0:T(8,128)(2,1)S(1)} %get-tuple-element.31.x_ref), channel_id=1, source_target_pairs={{0,1},{1,0},{2,3},{3,2},{4,5},{5,4},{6,7},{7,6},{8,9},{9,8},{10,11... | collective-permute-start | bytes 2359304 | tf_op jit(solution)/shard_map/ppermute | solution.py:198
  3.0 14.0 %collective-permute-start.6 = (bf16[96,1024]{1,0:T(8,128)(2,1)S(1)}, bf16[96,1024]{1,0:T(8,128)(2,1)S(1)}, u32[]{:S(2)}, u32[]{:S(2)}) collective-permute-start(bf16[96,1024]{1,0:T(8,128)(2,1)S(1)} %get-tuple-element.36), channel_id=1, source_target_pairs={{0,128},{1,129},{2,130},{3,131},{4,132},{5,133},{6,134},{7,135},{8... | collective-permute-start | bytes 589832 | tf_op jit(solution)/shard_map/ppermute | solution.py:197
  3.1 21.6 %collective-permute-start.4 = (bf16[96,1024]{1,0:T(8,128)(2,1)S(1)}, bf16[96,1024]{1,0:T(8,128)(2,1)S(1)}, u32[]{:S(2)}, u32[]{:S(2)}) collective-permute-start(bf16[96,1024]{1,0:T(8,128)(2,1)S(1)} %get-tuple-element.35), channel_id=1, source_target_pairs={{0,128},{1,129},{2,130},{3,131},{4,132},{5,133},{6,134},{7,135},{8... | collective-permute-start | bytes 589832 | tf_op jit(solution)/shard_map/ppermute | solution.py:197
  5.1 19.7 %collective-permute-start.2 = (bf16[96,1024]{1,0:T(8,128)(2,1)S(1)}, bf16[96,1024]{1,0:T(8,128)(2,1)S(1)}, u32[]{:S(2)}, u32[]{:S(2)}) collective-permute-start(bf16[96,1024]{1,0:T(8,128)(2,1)S(1)} %get-tuple-element.34), channel_id=1, source_target_pairs={{0,128},{1,129},{2,130},{3,131},{4,132},{5,133},{6,134},{7,135},{8... | collective-permute-start | bytes 589832 | tf_op jit(solution)/shard_map/ppermute | solution.py:197
  5.2 26.7 %collective-permute-start = (bf16[96,1024]{1,0:T(8,128)(2,1)S(1)}, bf16[96,1024]{1,0:T(8,128)(2,1)S(1)}, u32[]{:S(2)}, u32[]{:S(2)}) collective-permute-start(bf16[96,1024]{1,0:T(8,128)(2,1)S(1)} %get-tuple-element.33), channel_id=1, source_target_pairs={{0,128},{1,129},{2,130},{3,131},{4,132},{5,133},{6,134},{7,135},{8... | collective-permute-start | bytes 589832 | tf_op jit(solution)/shard_map/ppermute | solution.py:197
  9.5 1.6 %copy-start = (bf16[1024,1024]{1,0:T(8,128)(2,1)S(1)}, bf16[1024,1024]{1,0:T(8,128)(2,1)}, u32[]{:S(2)}) copy-start(bf16[1024,1024]{1,0:T(8,128)(2,1)} %refs_1_.17) | copy-start | bytes 6291460
  11.1 1.6 %copy-start.2 = (bf16[1024,1024]{1,0:T(8,128)(2,1)S(1)}, bf16[1024,1024]{1,0:T(8,128)(2,1)}, u32[]{:S(2)}) copy-start(bf16[1024,1024]{1,0:T(8,128)(2,1)} %refs_2_.17) | copy-start | bytes 6291460
  12.7 1.6 %copy-start.9 = (bf16[1024,1024]{1,0:T(8,128)(2,1)S(1)}, bf16[1024,1024]{1,0:T(8,128)(2,1)}, u32[]{:S(2)}) copy-start(bf16[1024,1024]{1,0:T(8,128)(2,1)} %wq_ref.1) | copy-start | bytes 6291460
  14.3 17.9 %copy-start.1 = (bf16[1024,1024]{1,0:T(8,128)(2,1)S(1)}, bf16[1024,1024]{1,0:T(8,128)(2,1)}, u32[]{:S(2)}) copy-start(bf16[1024,1024]{1,0:T(8,128)(2,1)} %refs_1_.17) | copy-start | bytes 6291460
  17.0 18.6 %collective-permute-start.7 = (bf16[96,1024]{1,0:T(8,128)(2,1)S(1)}, bf16[96,1024]{1,0:T(8,128)(2,1)S(1)}, u32[]{:S(2)}, u32[]{:S(2)}) collective-permute-start(bf16[96,1024]{1,0:T(8,128)(2,1)S(1)} %collective-permute-done.6.refs_0_), channel_id=1, source_target_pairs={{0,255},{1,130},{2,129},{3,132},{4,131},{5,134},{6,133},{7,136},{8... | collective-permute-start | bytes 589832 | tf_op jit(solution)/shard_map/ppermute | solution.py:199
  24.7 12.5 %collective-permute-start.5 = (bf16[96,1024]{1,0:T(8,128)(2,1)S(1)}, bf16[96,1024]{1,0:T(8,128)(2,1)S(1)}, u32[]{:S(2)}, u32[]{:S(2)}) collective-permute-start(bf16[96,1024]{1,0:T(8,128)(2,1)S(1)} %collective-permute-done.4.refs_0_), channel_id=1, source_target_pairs={{0,255},{1,130},{2,129},{3,132},{4,131},{5,134},{6,133},{7,136},{8... | collective-permute-start | bytes 589832 | tf_op jit(solution)/shard_map/ppermute | solution.py:199
  24.8 14.0 %collective-permute-start.3 = (bf16[96,1024]{1,0:T(8,128)(2,1)S(1)}, bf16[96,1024]{1,0:T(8,128)(2,1)S(1)}, u32[]{:S(2)}, u32[]{:S(2)}) collective-permute-start(bf16[96,1024]{1,0:T(8,128)(2,1)S(1)} %collective-permute-done.2.refs_0_), channel_id=1, source_target_pairs={{0,255},{1,130},{2,129},{3,132},{4,131},{5,134},{6,133},{7,136},{8... | collective-permute-start | bytes 589832 | tf_op jit(solution)/shard_map/ppermute | solution.py:199
  31.9 13.9 %collective-permute-start.1 = (bf16[96,1024]{1,0:T(8,128)(2,1)S(1)}, bf16[96,1024]{1,0:T(8,128)(2,1)S(1)}, u32[]{:S(2)}, u32[]{:S(2)}) collective-permute-start(bf16[96,1024]{1,0:T(8,128)(2,1)S(1)} %collective-permute-done.refs_0_), channel_id=1, source_target_pairs={{0,255},{1,130},{2,129},{3,132},{4,131},{5,134},{6,133},{7,136},{8... | collective-permute-start | bytes 589832 | tf_op jit(solution)/shard_map/ppermute | solution.py:199
  38.9 1.6 %copy-start.4 = (bf16[1024,1024]{1,0:T(8,128)(2,1)S(1)}, bf16[1024,1024]{1,0:T(8,128)(2,1)}, u32[]{:S(2)}) copy-start(bf16[1024,1024]{1,0:T(8,128)(2,1)} %wo_ref.3) | copy-start | bytes 6291460
  38.9 1.6 %copy-start.8 = (s32[1,3]{1,0:T(1,128)S(1)}, s32[1,3]{1,0:T(1,128)}, u32[]{:S(2)}) copy-start(s32[1,3]{1,0:T(1,128)} %param.18) | copy-start | bytes 40
  40.5 5.4 %copy-start.3 = (bf16[1024,1024]{1,0:T(8,128)(2,1)S(1)}, bf16[1024,1024]{1,0:T(8,128)(2,1)}, u32[]{:S(2)}) copy-start(bf16[1024,1024]{1,0:T(8,128)(2,1)} %refs_2_.17) | copy-start | bytes 6291460

commit v2 on v1

v2 whole, which is shorter than its diff:
```python
import functools
import math

import jax
import jax.numpy as jnp
import numpy as np
from jax import lax
from jax.experimental import pallas as pl
from jax.experimental.pallas import tpu as pltpu
from jax.sharding import PartitionSpec as P

HEADS = 16
NS = 6
CS = 4
SLOTS = NS + CS
BT = 64
NBLK = 3
D = 1024
HEAD = D // HEADS
GROUP = 4
GW = GROUP * HEAD
TOK = NBLK * BT
ROWS = 2 * TOK
CHUNKS = 3
CR = ROWS // CHUNKS
STEP = math.gcd(CR, TOK)
BOTH = ("frame", "tile")
VMEM = pl.BlockSpec(memory_space=pltpu.VMEM)
ANY = pl.BlockSpec(memory_space=pl.ANY)
EXP_SCALE = float(np.log2(np.e) / np.sqrt(HEAD))


def params(limit):
    return pltpu.CompilerParams(vmem_limit_bytes=limit)


def in_hbm(x):
    return pltpu.with_memory_space_constraint(x, pltpu.HBM)


def cost(flops, nbytes):
    return pl.CostEstimate(flops=int(flops), bytes_accessed=int(nbytes), transcendentals=0)


def norm_kernel(tok_hbm, gain_hbm, mod_hbm, whole_ref, *rest):
    chunk_refs, (tok_ref, gain_ref, mod_ref, sems) = rest[:CHUNKS], rest[CHUNKS:]
    side = [
        pltpu.make_async_copy(gain_hbm, gain_ref, sems.at[ROWS // STEP]),
        pltpu.make_async_copy(mod_hbm, mod_ref, sems.at[ROWS // STEP + 1]),
    ]
    loads = []
    for i in range(ROWS // STEP):
        frame, row = divmod(i * STEP, TOK)
        rows = pl.ds(row, STEP)
        loads.append(
            pltpu.make_async_copy(tok_hbm.at[frame, rows], tok_ref.at[frame, rows], sems.at[i])
        )
    for copy in loads[:1] + side + loads[1:]:
        copy.start()
    for copy in side:
        copy.wait()
    for i in range(ROWS // STEP):
        frame, row = divmod(i * STEP, TOK)
        loads[i].wait()
        x = tok_ref[frame, row : row + STEP, :].astype(jnp.float32)
        meansq = jnp.mean(x * x, axis=-1, keepdims=True)
        scaled = x * lax.rsqrt(meansq + 1e-06) * gain_ref[...] * (1.0 + mod_ref[frame : frame + 1, :])
        normed = scaled.astype(jnp.bfloat16)
        whole_ref[i * STEP : (i + 1) * STEP, :] = normed
        chunk, row = divmod(i * STEP, CR)
        chunk_refs[chunk][row : row + STEP, :] = normed


def norm(tokens, gain, mod):
    chunk = jax.ShapeDtypeStruct((CR, D), jnp.bfloat16)
    return pl.pallas_call(
        norm_kernel,
        out_shape=[jax.ShapeDtypeStruct((ROWS, D), jnp.bfloat16)] + [chunk] * CHUNKS,
        in_specs=[ANY] * 3,
        out_specs=[VMEM] * (1 + CHUNKS),
        scratch_shapes=[
            pltpu.VMEM((2, TOK, D), jnp.bfloat16),
            pltpu.VMEM((1, D), jnp.float32),
            pltpu.VMEM((2, D), jnp.float32),
            pltpu.SemaphoreType.DMA((ROWS // STEP + 2,)),
        ],
        compiler_params=params(8 << 20),
        cost_estimate=cost(ROWS * D * 8, ROWS * D * 6),
    )(*map(in_hbm, (tokens, gain, mod)))


def project_into(x, w_ref, out_ref, at, width=256):
    rows = x.shape[0]
    for c in range(0, D, width):
        out_ref[at : at + rows, c : c + width] = jnp.dot(
            x, w_ref[:, c : c + width], preferred_element_type=jnp.float32
        ).astype(jnp.bfloat16)


def own_kernel(x_ref, wk_hbm, wv_hbm, wq_hbm, *refs):
    k_ref, v_ref, q_ref, wk_ref, wv_ref, wq_ref, sems = refs[-7:]
    steps = ((wq_hbm, wq_ref, q_ref), (wk_hbm, wk_ref, k_ref), (wv_hbm, wv_ref, v_ref))
    loads = [
        pltpu.make_async_copy(hbm, vmem, sems.at[i]) for i, (hbm, vmem, _) in enumerate(steps)
    ]
    for copy in loads[:2]:
        copy.start()
    for i, (_, w_ref, out_ref) in enumerate(steps):
        loads[i].wait()
        if i + 2 < len(loads):
            loads[i + 2].start()
        project_into(x_ref[...], w_ref, out_ref, 0)


def own_project(x, wq, wk, wv, later):
    n = len(later)
    rows = pltpu.VMEM((ROWS, D), jnp.bfloat16)
    weight = pltpu.VMEM((D, D), jnp.bfloat16)
    return pl.pallas_call(
        own_kernel,
        out_shape=[jax.ShapeDtypeStruct(c.shape, c.dtype) for c in later] + [rows] * 3 + [weight] * 2,
        in_specs=[VMEM] + [ANY] * 3 + [VMEM] * n,
        out_specs=[VMEM] * (n + 5),
        input_output_aliases={4 + i: i for i in range(n)},
        scratch_shapes=[pltpu.VMEM((D, D), jnp.bfloat16), pltpu.SemaphoreType.DMA((3,))],
        compiler_params=params(12 << 20),
        cost_estimate=cost(6 * ROWS * D * D, 6 * D * D),
    )(x, *map(in_hbm, (wk, wv, wq)), *later)


def gate_kernel(*refs):
    pass


def gate(x, after):
    return pl.pallas_call(
        gate_kernel,
        out_shape=jax.ShapeDtypeStruct(x.shape, x.dtype),
        in_specs=[VMEM] * 2,
        out_specs=VMEM,
        input_output_aliases={0: 0},
        compiler_params=params(1 << 20),
    )(x, after)


def kv_kernel(ats, n_copies, *refs):
    n = len(ats)
    wk_ref, wv_ref = refs[n : n + 2]
    sources = refs[n + 2 : n + 2 + len(n_copies)]
    k_ref, v_ref, token_ref = refs[-4:-1] if n_copies else refs[-3:]
    token_ref[...] = jnp.zeros_like(token_ref)
    copies = []
    for source, (side, at) in zip(sources, n_copies):
        target = (k_ref, v_ref)[side].at[pl.ds(at, ROWS)]
        copies.append(pltpu.make_async_copy(source, target, refs[-1].at[len(copies)]))
        copies[-1].start()
    x = jnp.concatenate([ref[...] for ref in refs[:n]], axis=0) if n > 1 else refs[0][...]
    for w_ref, out_ref in ((wk_ref, k_ref), (wv_ref, v_ref)):
        for c in range(0, D, 256):
            y = jnp.dot(x, w_ref[:, c : c + 256], preferred_element_type=jnp.float32).astype(jnp.bfloat16)
            row = 0
            for ref, at in zip(refs[:n], ats):
                rows = ref.shape[0]
                out_ref[at : at + rows, c : c + 256] = y[row : row + rows]
                row += rows
    for copy in copies:
        copy.wait()


def kv_project(xs, ats, wk, wv, held=None, copied=()):
    n, m = len(xs), len(copied)
    rows = sum(x.shape[0] for x in xs)
    shape = pltpu.VMEM((4 * ROWS, D), jnp.bfloat16)
    extra = [] if held is None else list(held)
    return pl.pallas_call(
        functools.partial(kv_kernel, ats, [c[1:] for c in copied]),
        out_shape=[shape, shape, jax.ShapeDtypeStruct((8, 128), jnp.float32)],
        in_specs=[VMEM] * (n + 2 + m + len(extra)),
        out_specs=[VMEM] * 3,
        input_output_aliases={n + 2 + m: 0, n + 3 + m: 1} if extra else {},
        scratch_shapes=[pltpu.SemaphoreType.DMA((m,))] if m else [],
        compiler_params=params(8 << 20),
        cost_estimate=cost(4 * rows * D * D, 6 * D * D),
    )(*xs, wk, wv, *[c[0] for c in copied], *extra)


def attend_kernel(frame, *refs):
    neigh_hbm, count_hbm, cross_hbm, q_ref, k_ref, v_ref, wo_hbm = refs[:7]
    out_ref, wo_ref, att_ref, upd_ref, neigh_ref, count_ref, cross_ref, sems = refs[-8:]
    lists = [
        pltpu.make_async_copy(neigh_hbm, neigh_ref, sems.at[0]),
        pltpu.make_async_copy(count_hbm, count_ref, sems.at[1]),
        pltpu.make_async_copy(cross_hbm, cross_ref, sems.at[2]),
    ]
    wo_copy = pltpu.make_async_copy(wo_hbm, wo_ref, sems.at[4])
    for copy in lists + [wo_copy]:
        copy.start()
    for copy in lists:
        copy.wait()
    mine = lax.axis_index("frame")
    odd = lax.axis_index("tile") % 2
    r = lax.broadcasted_iota(jnp.int32, (GW, GW), 0) // HEAD
    c = lax.broadcasted_iota(jnp.int32, (GW, GW), 1) // HEAD
    diagonal = r == c
    lane = lax.broadcasted_iota(jnp.int32, (1, SLOTS * BT), 1) // BT

    def rows_of(block):
        return pl.ds(pl.multiple_of(block * BT, BT), BT)

    def slots(b):
        found = []
        for s in range(NS):
            e = neigh_ref[0, b, s]
            side = e // NBLK
            core = jnp.where(side == 2, odd == 0, odd == 1)
            source = jnp.where(side == 1, 0, jnp.where(core, 2, 3))
            found.append(source * (2 * NBLK) + frame * NBLK + (e - side * NBLK))
        for s in range(CS):
            e = cross_ref[frame, 0, b, s]
            owner = e // (2 * NBLK)
            found.append(e - owner * (2 * NBLK) + jnp.where(owner == mine, 0, 2 * NBLK))
        return [rows_of(f) for f in found]

    def block(b, g, at):
        u = frame * NBLK + b
        cols = slice(g * GW, (g + 1) * GW)
        q = q_ref[u * BT : (u + 1) * BT, cols]
        q4 = jnp.concatenate([q] * GROUP, axis=0)
        q4 = jnp.where(diagonal, q4, jnp.zeros_like(q4))
        keys = jnp.concatenate([k_ref[a, cols] for a in at], axis=0)
        values = jnp.concatenate([v_ref[a, cols] for a in at], axis=0)
        scores = lax.dot_general(
            q4, keys, (((1,), (1,)), ((), ())), preferred_element_type=jnp.float32
        )
        unused = (lane >= count_ref[0, b]) & (lane < NS)
        scores = scores + jnp.where(unused, jnp.float32(-1e30), jnp.float32(0.0))
        peak = jnp.max(scores, axis=1, keepdims=True)
        weights = jnp.exp2((scores - peak) * EXP_SCALE)
        total = jnp.sum(weights, axis=1, keepdims=True)
        weights = (weights * (1.0 / total)).astype(jnp.bfloat16)
        att = jnp.dot(weights, values, preferred_element_type=jnp.float32)
        att = jnp.where(diagonal, att, 0.0)
        att = sum(att[h * BT : (h + 1) * BT] for h in range(GROUP))
        att_ref[b * BT : (b + 1) * BT, cols] = att.astype(jnp.bfloat16)

    at = [slots(b) for b in range(NBLK)]
    for g in range(D // GW):
        for b in range(NBLK):
            block(b, g, at[b])
    wo_copy.wait()
    project_into(att_ref[...], wo_ref, upd_ref, 0)
    copy = pltpu.make_async_copy(upd_ref, out_ref.at[frame], sems.at[3])
    copy.start()
    copy.wait()


def attend(frame, lists, queries, keys, values, w_out, earlier=None):
    extra = [] if earlier is None else [earlier]
    return pl.pallas_call(
        functools.partial(attend_kernel, frame),
        out_shape=jax.ShapeDtypeStruct((2, TOK, D), jnp.bfloat16),
        in_specs=[ANY] * 3 + [VMEM] * 3 + [ANY] * (1 + len(extra)),
        out_specs=ANY,
        scratch_shapes=[
            pltpu.VMEM((D, D), jnp.bfloat16),
            pltpu.VMEM((TOK, D), jnp.bfloat16),
            pltpu.VMEM((TOK, D), jnp.bfloat16),
        ]
        + [pltpu.SMEM(x.shape, jnp.int32) for x in lists]
        + [pltpu.SemaphoreType.DMA((5,))],
        input_output_aliases={7: 0} if extra else {},
        compiler_params=params(16 << 20),
        cost_estimate=cost(2 * TOK * D * D + 16 * TOK * SLOTS * BT * D, 8 * D * D),
    )(*lists, queries, keys, values, in_hbm(w_out), *extra)


def local(tokens, norm_gain, modulation, w_query, w_key, w_value, w_out, neigh_list, neigh_count, cross_list):
    tiles = lax.axis_size("tile")

    def device(f, t):
        return f * tiles + t % tiles

    cells = [(f, t) for f in range(2) for t in range(tiles)]
    partner = [(device(f, t), device(1 - f, t)) for f, t in cells]
    pair = [(device(f, t), device(f, t ^ 1)) for f, t in cells]
    onward = [(device(f, t), device(1 - f, t + 1 if t % 2 else t - 1)) for f, t in cells]

    def swap(x):
        return lax.ppermute(x, BOTH, partner)

    def cross(x):
        return lax.ppermute(x, BOTH, pair)

    def forward(x):
        return lax.ppermute(x, BOTH, onward)

    lists = (neigh_list, neigh_count, cross_list)
    whole, *chunks = norm(tokens, norm_gain[None], modulation)
    across = cross(whole)
    *later, own_k, own_v, queries, wk, wv = own_project(whole, w_query, w_key, w_value, chunks[2:])
    swapped = [swap(c) for c in chunks[:2] + later]

    def at(source, i):
        return source * ROWS + i * CR

    beyond, held = [], None
    for i, arrived in enumerate(swapped):
        if held is not None:
            arrived = gate(arrived, token)
        beyond.append(forward(arrived))
        if i == 0:
            *held, token = kv_project(
                [across, arrived], [2 * ROWS, at(1, 0)], wk, wv, None, [(own_k, 0, 0), (own_v, 1, 0)]
            )
        else:
            *held, token = kv_project([arrived, beyond[i - 1]], [at(1, i), at(3, i - 1)], wk, wv, held)
    first = attend(0, lists, queries, *held, w_out)
    *held, _ = kv_project([beyond[-1]], [at(3, CHUNKS - 1)], wk, wv, held)
    return attend(1, lists, queries, *held, w_out, first)


def solution(mesh):
    return jax.shard_map(
        local,
        mesh=mesh,
        in_specs=(
            P("frame", "tile", None),
            P(),
            P("frame", None),
            P(),
            P(),
            P(),
            P(),
            P("tile", None, None),
            P("tile", None),
            P("frame", "tile", None, None),
        ),
        out_specs=P("frame", "tile", None),
        check_vma=False,
    )
```

time: 52.5 us -> 47.3 us (0.901)
  local copies, waits for them, and re-layouts: 8.17 us -> 0.01 us
  waiting for transfers between devices: 0.02 us -> 3.36 us
  Pallas kernels: 21.9 us -> 24.6 us
  other arithmetic: 2.26 us -> 0 us
    unnamed x21 -> x8, local copies, waits for them, and re-layouts: 8.08 us -> 0.01 us
    ppermute x9 -> x7, waiting for transfers between devices: 0.02 us -> 3.36 us  [the longest x3 2.3 us: swap(): return lax.ppermute(x, BOTH, partner)]
    pallas_call x1, Pallas kernels: 0.37 us -> 1.78 us  [norm(): pl.pallas_call(norm_kernel, out_shape=[jax.ShapeDtypeStruct((ROWS, D), jn...]
    pallas_call x2, Pallas kernels: 10.7 us -> 11.5 us  [attend(): pl.pallas_call(functools.partial(attend_kernel, frame), out_shape=jax.Sha...]
    add x3 -> x0, other arithmetic: 0.78 us -> none  [the longest x1 0.7 us: slot_table(): near = source * 2 * NBLK + neigh % NBLK]
    div x1 -> x0, other arithmetic: 0.7 us -> none  [slot_table(): owner = cross // (2 * NBLK)]
    ne x1 -> x0, other arithmetic: 0.7 us -> none  [slot_table(): owner = cross // (2 * NBLK)]
    ppermute x9 -> x7, starting transfers between devices: 19.4 us -> 19 us  [the longest x3 16.6 us: forward(): return lax.ppermute(x, BOTH, onward)]
  transfers between devices with their start and end apart: 9 -> 7, of which waited for: 0 -> 2; matrix products, arithmetic and copies ran while one was open for 5% -> 0% of each run, Pallas kernels for 30% -> 34%
where the time goes in v2:
time: 47.3 us; the launch traced here: 47.2 us
  Pallas kernels  24.6 us (52%)
  starting transfers between devices  19 us (40%)
  waiting for transfers between devices  3.36 us (7%)
    ppermute x3, starting transfers between devices, forward(): return lax.ppermute(x, BOTH, onward)  16.6 us
    pallas_call x2, Pallas kernels, attend(): pl.pallas_call(functools.partial(attend_kernel, frame), out_shape=jax.Sha...  11.5 us
    pallas_call x4, Pallas kernels, kv_project(): pl.pallas_call(functools.partial(kv_kernel, ats, [c[1:] for c in copied])...  6.69 us
    pallas_call x1, Pallas kernels, own_project(): pl.pallas_call(own_kernel, out_shape=[jax.ShapeDtypeStruct(c.shape, c.dty...  4.59 us
    ppermute x3, waiting for transfers between devices, swap(): return lax.ppermute(x, BOTH, partner)  2.3 us
    ppermute x3, starting transfers between devices, swap(): return lax.ppermute(x, BOTH, partner)  2.3 us
    pallas_call x1, Pallas kernels, norm(): pl.pallas_call(norm_kernel, out_shape=[jax.ShapeDtypeStruct((ROWS, D), jn...  1.78 us
    ppermute x3, waiting for transfers between devices, forward(): return lax.ppermute(x, BOTH, onward)  1.05 us
  transfers between devices with their start and end apart: 7, of which 2 were waited for; matrix products, arithmetic and copies ran while one was open for 0% of the time, Pallas kernels for 34%

profile of v2, /device:TPU:0, one launch (start us, length us, event | category | flops | bytes accessed | tf_op | source)
XLA Modules:
  0.0 47.2 jit_solution(10495327044226955408)
XLA Ops:
  0.0 1.8 %shard_map.100 = (bf16[384,1024]{1,0:T(8,128)(2,1)S(1)}, bf16[128,1024]{1,0:T(8,128)(2,1)S(1)}, bf16[128,1024]{1,0:T(8,128)(2,1)S(1)}, bf16[128,1024]{1,0:T(8,128)(2,1)S(1)}) custom-call(bf16[2,192,1024]{2,1,0:T(8,128)(2,1)} %tok_hbm.1, f32[1,1024]{1,0:T(1,128)} %bitcast.1, f32[2,1024]{1,0:T(2,128)} %mod_hbm.1), custom_call_target="tpu_custom_call" | custom-call | flops 3145728 | bytes 2359296 | tf_op jit(solution)/shard_map/pallas_call | solution.py:76
  1.8 0.1 collective-permute-start.2
  1.9 0.1 collective-permute-start.3
  2.0 2.0 %collective-permute-start.1 = (bf16[128,1024]{1,0:T(8,128)(2,1)S(1)}, bf16[128,1024]{1,0:T(8,128)(2,1)S(1)}, u32[]{:S(2)}, u32[]{:S(2)}) collective-permute-start(bf16[128,1024]{1,0:T(8,128)(2,1)S(1)} %get-tuple-element.29), channel_id=1, source_target_pairs={{0,128},{1,129},{2,130},{3,131},{4,132},{5,133},{6,134},{7,135},{8... | collective-permute-start | bytes 786440 | tf_op jit(solution)/shard_map/ppermute | solution.py:289
  4.0 4.6 %shard_map.101 = (bf16[128,1024]{1,0:T(8,128)(2,1)S(1)}, bf16[384,1024]{1,0:T(8,128)(2,1)S(1)}, bf16[384,1024]{1,0:T(8,128)(2,1)S(1)}, bf16[384,1024]{1,0:T(8,12...) custom-call(bf16[384,1024]{1,0:T(8,128)(2,1)S(1)} %get-tuple-element., ...), custom_call_target="tpu_custom_call", output_to_operand_aliasing={{0}: (4, {})} | custom-call | flops 2415919104 | bytes 6291456 | tf_op jit(solution)/shard_map/pallas_call | solution.py:119
  8.6 0.2 collective-permute-start
  8.8 2.3 %collective-permute-done.3.refs_1_ = bf16[128,1024]{1,0:T(8,128)(2,1)S(1)} collective-permute-done((bf16[128,1024]{1,0:T(8,128)(2,1)S(1)}, bf16[128,1024]{1,0:T(8,128)(2,1)S(1)}, u32[]{:S(2)}, u32[]{:S(2)}) %collective-permute-start.3) | collective-permute-done | bytes 262176 | tf_op jit(solution)/shard_map/ppermute | solution.py:289
  11.1 7.5 %collective-permute-start.4 = (bf16[128,1024]{1,0:T(8,128)(2,1)S(1)}, bf16[128,1024]{1,0:T(8,128)(2,1)S(1)}, u32[]{:S(2)}, u32[]{:S(2)}) collective-permute-start(bf16[128,1024]{1,0:T(8,128)(2,1)S(1)} %collective-permute-done.3.refs_1_), channel_id=1, source_target_pairs={{0,255},{1,130},{2,129},{3,132},{4,131},{5,134},{6,133},{7,136},{8... | collective-permute-start | bytes 786440 | tf_op jit(solution)/shard_map/ppermute | solution.py:295
  18.6 0.0 collective-permute-done.2.refs_0_
  18.6 0.0 copy-start.2
  18.6 0.0 copy-start.1
  18.6 2.5 %shard_map.102 = (bf16[1536,1024]{1,0:T(8,128)(2,1)S(1)}, bf16[1536,1024]{1,0:T(8,128)(2,1)S(1)}, f32[8,128]{1,0:T(8,128)S(1)}) custom-call(bf16[384,1024]{1,0:T(8,128)(2,1)S(1)} %collective-permute-done.2.refs_0_, bf16[128,1024]{1,0:T(8,128)(2,1)S(1)} %collective-permute-done.3.refs_1_, bf16[1024,1024]{1,0:T(8,128)(2,1)S(1)} %get-tuple-element.31.refs_2_.refs_1_, ...), custom_call_target="tpu_custom_call" | custom-call | flops 2147483648 | bytes 6291456 | tf_op jit(solution)/shard_map/pallas_call | solution.py:175
  21.1 0.0 collective-permute-done.1.refs_0_
  21.1 3.1 %collective-permute-start.6 = (bf16[128,1024]{1,0:T(8,128)(2,1)S(1)}, bf16[128,1024]{1,0:T(8,128)(2,1)S(1)}, u32[]{:S(2)}, u32[]{:S(2)}) collective-permute-start(bf16[128,1024]{1,0:T(8,128)(2,1)S(1)} %shard_map.103.refs_0_), channel_id=1, source_target_pairs={{0,255},{1,130},{2,129},{3,132},{4,131},{5,134},{6,133},{7,136},{8... | collective-permute-start | bytes 786440 | tf_op jit(solution)/shard_map/ppermute | solution.py:295
  24.2 0.0 copy-done.2
  24.2 0.0 copy-done.1
  24.3 0.0 collective-permute-done.4.refs_1_
  24.3 1.3 %shard_map.104 = (bf16[1536,1024]{1,0:T(8,128)(2,1)S(1)}, bf16[1536,1024]{1,0:T(8,128)(2,1)S(1)}, f32[8,128]{1,0:T(8,128)S(1)}) custom-call(bf16[128,1024]{1,0:T(8,128)(2,1)S(1)} %shard_map.103.refs_0_, bf16[128,1024]{1,0:T(8,128)(2,1)S(1)} %collective-permute-done.4.refs_1_, ...), custom_call_target="tpu_custom_call", output_to_operand_aliasing={{0}: (4, {}), {1}: (5, {})} | custom-call | flops 1073741824 | bytes 6291456 | tf_op jit(solution)/shard_map/pallas_call | solution.py:175
  25.5 0.0 collective-permute-done.refs_0_
  25.6 6.0 %collective-permute-start.5 = (bf16[128,1024]{1,0:T(8,128)(2,1)S(1)}, bf16[128,1024]{1,0:T(8,128)(2,1)S(1)}, u32[]{:S(2)}, u32[]{:S(2)}) collective-permute-start(bf16[128,1024]{1,0:T(8,128)(2,1)S(1)} %shard_map.105.refs_0_), channel_id=1, source_target_pairs={{0,255},{1,130},{2,129},{3,132},{4,131},{5,134},{6,133},{7,136},{8... | collective-permute-start | bytes 786440 | tf_op jit(solution)/shard_map/ppermute | solution.py:295
  31.5 1.0 %collective-permute-done.6.refs_1_ = bf16[128,1024]{1,0:T(8,128)(2,1)S(1)} collective-permute-done((bf16[128,1024]{1,0:T(8,128)(2,1)S(1)}, bf16[128,1024]{1,0:T(8,128)(2,1)S(1)}, u32[]{:S(2)}, u32[]{:S(2)}) %collective-permute-start.6) | collective-permute-done | bytes 262176 | tf_op jit(solution)/shard_map/ppermute | solution.py:295
  32.6 0.0 copy-start
  32.6 1.7 %shard_map.106 = (bf16[1536,1024]{1,0:T(8,128)(2,1)S(1)}, bf16[1536,1024]{1,0:T(8,128)(2,1)S(1)}, f32[8,128]{1,0:T(8,128)}) custom-call(bf16[128,1024]{1,0:T(8,128)(2,1)S(1)} %shard_map.105.refs_0_, bf16[128,1024]{1,0:T(8,128)(2,1)S(1)} %collective-permute-done.6.refs_1_, ...), custom_call_target="tpu_custom_call", output_to_operand_aliasing={{0}: (4, {}), {1}: (5, {})} | custom-call | flops 1073741824 | bytes 6291456 | tf_op jit(solution)/shard_map/pallas_call | solution.py:175
  34.3 0.0 copy-done
  34.3 5.8 %shard_map.108.refs_7_ = bf16[2,192,1024]{2,1,0:T(8,128)(2,1)} custom-call(s32[1,3,6]{2,1,0:T(4,128)S(1)} %copy.23.refs_0_, s32[1,3]{1,0:T(1,128)S(1)} %copy-done, s32[2,1,3,4]{3,2,1,0:T(4,128)S(1)} %copy.24.refs_2_, bf16[384,1024]{1,0:T(8,128)(2,1)S(1)} %get-tuple-element.27.refs_3_, bf16[1536,1024]{1,0:T(8,128)(2,1)S(1)} %get-tuple-element.41.refs_3_.refs_4_, ...), custom_call_target="tpu_custom_call" | custom-call | flops 2415919104 | bytes 8388608 | tf_op jit(solution)/shard_map/pallas_call | solution.py:259
  40.1 0.0 collective-permute-done.5.refs_0_
  40.1 1.2 %shard_map.107 = (bf16[1536,1024]{1,0:T(8,128)(2,1)S(1)}, bf16[1536,1024]{1,0:T(8,128)(2,1)S(1)}, f32[8,128]{1,0:T(8,128)}) custom-call(bf16[128,1024]{1,0:T(8,128)(2,1)S(1)} %collective-permute-done.5.refs_0_, bf16[1024,1024]{1,0:T(8,128)(2,1)S(1)} %get-tuple-element.31.refs_2_.refs_1_, ...), custom_call_target="tpu_custom_call", output_to_operand_aliasing={{0}: (3, {}), {1}: (4, {})} | custom-call | flops 536870912 | bytes 6291456 | tf_op jit(solution)/shard_map/pallas_call | solution.py:175
  41.3 5.8 %shard_map.109 = bf16[2,192,1024]{2,1,0:T(8,128)(2,1)} custom-call(s32[1,3,6]{2,1,0:T(4,128)S(1)} %copy.23.refs_0_, s32[1,3]{1,0:T(1,128)S(1)} %copy-done, s32[2,1,3,4]{3,2,1,0:T(4,128)S(1)} %copy.24.refs_2_, bf16[384,1024]{1,0:T(8,128)(2,1)S(1)} %get-tuple-element.27.refs_3_, ...), custom_call_target="tpu_custom_call", output_to_operand_aliasing={{}: (7, {})} | custom-call | flops 2415919104 | bytes 8388608 | tf_op jit(solution)/shard_map/pallas_call | solution.py:259
  (4 shorter events, 0.0 us)
Async XLA Ops:
  1.8 16.8 %collective-permute-start.2 = (bf16[384,1024]{1,0:T(8,128)(2,1)S(1)}, bf16[384,1024]{1,0:T(8,128)(2,1)S(1)}, u32[]{:S(2)}, u32[]{:S(2)}) collective-permute-start(bf16[384,1024]{1,0:T(8,128)(2,1)S(1)} %get-tuple-element.25.x_ref), channel_id=1, source_target_pairs={{0,1},{1,0},{2,3},{3,2},{4,5},{5,4},{6,7},{7,6},{8,9},{9,8},{10,11... | collective-permute-start | bytes 2359304 | tf_op jit(solution)/shard_map/ppermute | solution.py:292
  1.9 9.2 %collective-permute-start.3 = (bf16[128,1024]{1,0:T(8,128)(2,1)S(1)}, bf16[128,1024]{1,0:T(8,128)(2,1)S(1)}, u32[]{:S(2)}, u32[]{:S(2)}) collective-permute-start(bf16[128,1024]{1,0:T(8,128)(2,1)S(1)} %get-tuple-element.30), channel_id=1, source_target_pairs={{0,128},{1,129},{2,130},{3,131},{4,132},{5,133},{6,134},{7,135},{8... | collective-permute-start | bytes 786440 | tf_op jit(solution)/shard_map/ppermute | solution.py:289
  2.0 19.1 %collective-permute-start.1 = (bf16[128,1024]{1,0:T(8,128)(2,1)S(1)}, bf16[128,1024]{1,0:T(8,128)(2,1)S(1)}, u32[]{:S(2)}, u32[]{:S(2)}) collective-permute-start(bf16[128,1024]{1,0:T(8,128)(2,1)S(1)} %get-tuple-element.29), channel_id=1, source_target_pairs={{0,128},{1,129},{2,130},{3,131},{4,132},{5,133},{6,134},{7,135},{8... | collective-permute-start | bytes 786440 | tf_op jit(solution)/shard_map/ppermute | solution.py:289
  8.6 16.9 %collective-permute-start = (bf16[128,1024]{1,0:T(8,128)(2,1)S(1)}, bf16[128,1024]{1,0:T(8,128)(2,1)S(1)}, u32[]{:S(2)}, u32[]{:S(2)}) collective-permute-start(bf16[128,1024]{1,0:T(8,128)(2,1)S(1)} %get-tuple-element.28), channel_id=1, source_target_pairs={{0,128},{1,129},{2,130},{3,131},{4,132},{5,133},{6,134},{7,135},{8... | collective-permute-start | bytes 786440 | tf_op jit(solution)/shard_map/ppermute | solution.py:289
  11.1 13.2 %collective-permute-start.4 = (bf16[128,1024]{1,0:T(8,128)(2,1)S(1)}, bf16[128,1024]{1,0:T(8,128)(2,1)S(1)}, u32[]{:S(2)}, u32[]{:S(2)}) collective-permute-start(bf16[128,1024]{1,0:T(8,128)(2,1)S(1)} %collective-permute-done.3.refs_1_), channel_id=1, source_target_pairs={{0,255},{1,130},{2,129},{3,132},{4,131},{5,134},{6,133},{7,136},{8... | collective-permute-start | bytes 786440 | tf_op jit(solution)/shard_map/ppermute | solution.py:295
  18.6 5.6 %copy-start.2 = (s32[1,3,6]{2,0,1:T(1,128)S(1)}, s32[1,3,6]{2,0,1:T(1,128)}, u32[]{:S(2)}) copy-start(s32[1,3,6]{2,0,1:T(1,128)} %param.17) | copy-start | bytes 220
  18.6 5.6 %copy-start.1 = (s32[2,1,3,4]{3,1,2,0:T(1,128)S(1)}, s32[2,1,3,4]{3,1,2,0:T(1,128)}, u32[]{:S(2)}) copy-start(s32[2,1,3,4]{3,1,2,0:T(1,128)} %param.19) | copy-start | bytes 292
  21.1 11.4 %collective-permute-start.6 = (bf16[128,1024]{1,0:T(8,128)(2,1)S(1)}, bf16[128,1024]{1,0:T(8,128)(2,1)S(1)}, u32[]{:S(2)}, u32[]{:S(2)}) collective-permute-start(bf16[128,1024]{1,0:T(8,128)(2,1)S(1)} %shard_map.103.refs_0_), channel_id=1, source_target_pairs={{0,255},{1,130},{2,129},{3,132},{4,131},{5,134},{6,133},{7,136},{8... | collective-permute-start | bytes 786440 | tf_op jit(solution)/shard_map/ppermute | solution.py:295
  25.6 14.5 %collective-permute-start.5 = (bf16[128,1024]{1,0:T(8,128)(2,1)S(1)}, bf16[128,1024]{1,0:T(8,128)(2,1)S(1)}, u32[]{:S(2)}, u32[]{:S(2)}) collective-permute-start(bf16[128,1024]{1,0:T(8,128)(2,1)S(1)} %shard_map.105.refs_0_), channel_id=1, source_target_pairs={{0,255},{1,130},{2,129},{3,132},{4,131},{5,134},{6,133},{7,136},{8... | collective-permute-start | bytes 786440 | tf_op jit(solution)/shard_map/ppermute | solution.py:295
  32.6 1.7 %copy-start = (s32[1,3]{1,0:T(1,128)S(1)}, s32[1,3]{1,0:T(1,128)}, u32[]{:S(2)}) copy-start(s32[1,3]{1,0:T(1,128)} %refs_1_.3) | copy-start | bytes 40

commit v3 on v2

v3 whole, which is shorter than its diff:
```python
import functools
import math

import jax
import jax.numpy as jnp
import numpy as np
from jax import lax
from jax.experimental import pallas as pl
from jax.experimental.pallas import tpu as pltpu
from jax.sharding import PartitionSpec as P

HEADS = 16
NS = 6
CS = 4
SLOTS = NS + CS
BT = 64
NBLK = 3
D = 1024
HEAD = D // HEADS
GROUP = 4
GW = GROUP * HEAD
TOK = NBLK * BT
ROWS = 2 * TOK
CHUNKS = 3
CR = ROWS // CHUNKS
STEP = math.gcd(CR, TOK)
BOTH = ("frame", "tile")
VMEM = pl.BlockSpec(memory_space=pltpu.VMEM)
ANY = pl.BlockSpec(memory_space=pl.ANY)
EXP_SCALE = float(np.log2(np.e) / np.sqrt(HEAD))


def params(limit):
    return pltpu.CompilerParams(vmem_limit_bytes=limit)


def in_hbm(x):
    return pltpu.with_memory_space_constraint(x, pltpu.HBM)


def cost(flops, nbytes):
    return pl.CostEstimate(flops=int(flops), bytes_accessed=int(nbytes), transcendentals=0)


def norm_kernel(tok_hbm, gain_hbm, mod_hbm, whole_ref, *rest):
    chunk_refs, (tok_ref, gain_ref, mod_ref, sems) = rest[:CHUNKS], rest[CHUNKS:]
    side = [
        pltpu.make_async_copy(gain_hbm, gain_ref, sems.at[ROWS // STEP]),
        pltpu.make_async_copy(mod_hbm, mod_ref, sems.at[ROWS // STEP + 1]),
    ]
    loads = []
    for i in range(ROWS // STEP):
        frame, row = divmod(i * STEP, TOK)
        rows = pl.ds(row, STEP)
        loads.append(
            pltpu.make_async_copy(tok_hbm.at[frame, rows], tok_ref.at[frame, rows], sems.at[i])
        )
    for copy in loads[:1] + side + loads[1:]:
        copy.start()
    for copy in side:
        copy.wait()
    for i in range(ROWS // STEP):
        frame, row = divmod(i * STEP, TOK)
        loads[i].wait()
        x = tok_ref[frame, row : row + STEP, :].astype(jnp.float32)
        meansq = jnp.mean(x * x, axis=-1, keepdims=True)
        scaled = x * lax.rsqrt(meansq + 1e-06) * gain_ref[...] * (1.0 + mod_ref[frame : frame + 1, :])
        normed = scaled.astype(jnp.bfloat16)
        whole_ref[i * STEP : (i + 1) * STEP, :] = normed
        chunk, row = divmod(i * STEP, CR)
        chunk_refs[chunk][row : row + STEP, :] = normed


def norm(tokens, gain, mod):
    chunk = jax.ShapeDtypeStruct((CR, D), jnp.bfloat16)
    return pl.pallas_call(
        norm_kernel,
        out_shape=[jax.ShapeDtypeStruct((ROWS, D), jnp.bfloat16)] + [chunk] * CHUNKS,
        in_specs=[ANY] * 3,
        out_specs=[VMEM] * (1 + CHUNKS),
        scratch_shapes=[
            pltpu.VMEM((2, TOK, D), jnp.bfloat16),
            pltpu.VMEM((1, D), jnp.float32),
            pltpu.VMEM((2, D), jnp.float32),
            pltpu.SemaphoreType.DMA((ROWS // STEP + 2,)),
        ],
        compiler_params=params(8 << 20),
        cost_estimate=cost(ROWS * D * 8, ROWS * D * 6),
    )(*map(in_hbm, (tokens, gain, mod)))


def project_into(x, w_ref, out_ref, at, width=256):
    rows = x.shape[0]
    for c in range(0, D, width):
        out_ref[at : at + rows, c : c + width] = jnp.dot(
            x, w_ref[:, c : c + width], preferred_element_type=jnp.float32
        ).astype(jnp.bfloat16)


def own_kernel(n, *refs):
    x_ref, hbms, refs = refs[0], refs[1:4], refs[4 + 2 * n :]
    out_refs, w_refs, sems = refs[:3], (refs[5], refs[3], refs[4]), refs[6]
    loads = [pltpu.make_async_copy(hbm, w, sems.at[i]) for i, (hbm, w) in enumerate(zip(hbms, w_refs))]
    for copy in loads[:2]:
        copy.start()
    for i, (w_ref, out_ref) in enumerate(zip(w_refs, out_refs)):
        loads[i].wait()
        if i + 2 < len(loads):
            loads[i + 2].start()
        project_into(x_ref[...], w_ref, out_ref, 0)


def own_project(x, weights, later=()):
    n = len(later)
    weight = pltpu.VMEM((D, D), jnp.bfloat16)
    out = pl.pallas_call(
        functools.partial(own_kernel, n),
        out_shape=[jax.ShapeDtypeStruct(c.shape, c.dtype) for c in later]
        + [pltpu.VMEM((ROWS, D), jnp.bfloat16)] * 3
        + [weight] * 2,
        in_specs=[VMEM] + [ANY] * 3 + [VMEM] * n,
        out_specs=[VMEM] * (n + 5),
        input_output_aliases={4 + i: i for i in range(n)},
        scratch_shapes=[weight, pltpu.SemaphoreType.DMA((3,))],
        compiler_params=params(12 << 20),
        cost_estimate=cost(6 * ROWS * D * D, 6 * D * D),
    )(x, *map(in_hbm, weights), *later)
    return out[:n], out[n : n + 3], out[n + 3 :]


def gate_kernel(*refs):
    pass


def gate(x, after):
    return pl.pallas_call(
        gate_kernel,
        out_shape=jax.ShapeDtypeStruct(x.shape, x.dtype),
        in_specs=[VMEM] * 2,
        out_specs=VMEM,
        input_output_aliases={0: 0},
        compiler_params=params(1 << 20),
    )(x, after)


def project_rows(x_refs, ats, pairs):
    x = jnp.concatenate([ref[...] for ref in x_refs], axis=0) if len(x_refs) > 1 else x_refs[0][...]
    for w_ref, out_ref in pairs:
        for c in range(0, D, 256):
            y = jnp.dot(x, w_ref[:, c : c + 256], preferred_element_type=jnp.float32).astype(jnp.bfloat16)
            row = 0
            for ref, at in zip(x_refs, ats):
                rows = ref.shape[0]
                out_ref[at : at + rows, c : c + 256] = y[row : row + rows]
                row += rows


def kv_kernel(ats, own, *refs):
    n = len(ats)
    wk_ref, wv_ref = refs[n : n + 2]
    k_ref, v_ref, token_ref = refs[n + 4 : n + 7]
    token_ref[...] = jnp.zeros_like(token_ref)
    copies = []
    if own:
        for i, (source, held_ref) in enumerate(zip(refs[n + 2 : n + 4], (k_ref, v_ref))):
            copies.append(pltpu.make_async_copy(source, held_ref.at[pl.ds(0, ROWS)], refs[-1].at[i]))
            copies[-1].start()
    project_rows(refs[:n], ats, ((wk_ref, k_ref), (wv_ref, v_ref)))
    for copy in copies:
        copy.wait()


def kv_project(xs, ats, wk, wv, held, own):
    n = len(xs)
    rows = sum(x.shape[0] for x in xs)
    shape = pltpu.VMEM((4 * ROWS, D), jnp.bfloat16)
    return pl.pallas_call(
        functools.partial(kv_kernel, ats, own),
        out_shape=[shape, shape, jax.ShapeDtypeStruct((8, 128), jnp.float32)],
        in_specs=[VMEM] * (n + 4),
        out_specs=[VMEM] * 3,
        input_output_aliases={} if own else {n + 2: 0, n + 3: 1},
        scratch_shapes=[pltpu.SemaphoreType.DMA((2,))] if own else [],
        compiler_params=params(8 << 20),
        cost_estimate=cost(4 * rows * D * D, 6 * D * D),
    )(*xs, wk, wv, *held)


def attend_kernel(ats, finish, *refs):
    refs = list(refs)

    def take(n):
        out = refs[:n]
        del refs[:n]
        return out

    x_refs = take(len(ats))
    wk_ref, wv_ref, q_ref, neigh_hbm, count_hbm, cross_hbm = take(6)
    take(2)
    if finish is not None:
        part_refs, (wo_hbm,) = take(3), take(1)
        take(finish)
    k_ref, v_ref = take(2)
    if finish is None:
        part_refs = take(3)
    else:
        (out_ref,) = take(1)
    neigh_ref, count_ref, cross_ref, sems = take(4)
    if finish is not None:
        wo_ref, att_ref, upd_ref = take(3)
    lists = [
        pltpu.make_async_copy(neigh_hbm, neigh_ref, sems.at[0]),
        pltpu.make_async_copy(count_hbm, count_ref, sems.at[1]),
        pltpu.make_async_copy(cross_hbm, cross_ref, sems.at[2]),
    ]
    for copy in lists:
        copy.start()
    if finish is not None:
        wo_copy = pltpu.make_async_copy(wo_hbm, wo_ref, sems.at[3])
        wo_copy.start()
    project_rows(x_refs, ats, ((wk_ref, k_ref), (wv_ref, v_ref)))
    for copy in lists:
        copy.wait()
    mine = lax.axis_index("frame")
    odd = lax.axis_index("tile") % 2
    r = lax.broadcasted_iota(jnp.int32, (GW, GW), 0) // HEAD
    c = lax.broadcasted_iota(jnp.int32, (GW, GW), 1) // HEAD
    diagonal = r == c
    even_head = lax.broadcasted_iota(jnp.int32, (BT, 2 * HEAD), 1) < HEAD
    lane = lax.broadcasted_iota(jnp.int32, (1, NS * BT), 1) // BT

    def rows_of(block):
        return pl.ds(pl.multiple_of(block * BT, BT), BT)

    def near_slots(frame, b):
        found = []
        for s in range(NS):
            e = neigh_ref[0, b, s]
            side = e // NBLK
            core = jnp.where(side == 2, odd == 0, odd == 1)
            source = jnp.where(side == 1, 0, jnp.where(core, 2, 3))
            found.append(rows_of(source * (2 * NBLK) + frame * NBLK + (e - side * NBLK)))
        return found

    def far_slots(frame, b):
        found = []
        for s in range(CS):
            e = cross_ref[frame, 0, b, s]
            owner = e // (2 * NBLK)
            found.append(rows_of(e - owner * (2 * NBLK) + jnp.where(owner == mine, 0, 2 * NBLK)))
        return found

    def own_columns(x):
        halves = []
        for h in range(0, GROUP, 2):
            two = slice(h * HEAD, (h + 2) * HEAD) if x.shape[1] > 1 else slice(0, 1)
            halves.append(
                jnp.where(even_head, x[h * BT : (h + 1) * BT, two], x[(h + 1) * BT : (h + 2) * BT, two])
            )
        return jnp.concatenate(halves, axis=1)

    def part(frame, b, g, at, masked):
        u = frame * NBLK + b
        cols = slice(g * GW, (g + 1) * GW)
        q = q_ref[u * BT : (u + 1) * BT, cols]
        q4 = jnp.concatenate([q] * GROUP, axis=0)
        q4 = jnp.where(diagonal, q4, jnp.zeros_like(q4))
        keys = jnp.concatenate([k_ref[a, cols] for a in at], axis=0)
        values = jnp.concatenate([v_ref[a, cols] for a in at], axis=0)
        scores = lax.dot_general(
            q4, keys, (((1,), (1,)), ((), ())), preferred_element_type=jnp.float32
        )
        if masked:
            scores = scores + jnp.where(lane < count_ref[0, b], jnp.float32(0.0), jnp.float32(-1e30))
        peak = jnp.max(scores, axis=1, keepdims=True)
        weights = jnp.exp2((scores - peak) * EXP_SCALE)
        total = jnp.sum(weights, axis=1, keepdims=True)
        att = jnp.dot(weights.astype(jnp.bfloat16), values, preferred_element_type=jnp.float32)
        return own_columns(att), own_columns(peak), own_columns(total)

    def parts(frame, slots, masked):
        at = [slots(frame, b) for b in range(NBLK)]
        for g in range(D // GW):
            for b in range(NBLK):
                where = (slice(b * BT, (b + 1) * BT), slice(g * GW, (g + 1) * GW))
                yield where, part(frame, b, g, at[b], masked)

    if finish is None:
        for frame in range(2):
            for where, values in parts(frame, far_slots, False):
                for ref, value in zip(part_refs, values):
                    ref[(frame, *where)] = value
        return
    for where, (att, peak, total) in parts(finish, near_slots, True):
        att2, peak2, total2 = (ref[(finish, *where)] for ref in part_refs)
        top = jnp.maximum(peak, peak2)
        scale, scale2 = jnp.exp2((peak - top) * EXP_SCALE), jnp.exp2((peak2 - top) * EXP_SCALE)
        whole = total * scale + total2 * scale2
        att_ref[where] = ((att * scale + att2 * scale2) / whole).astype(jnp.bfloat16)
    wo_copy.wait()
    copies = []
    for i, col in enumerate(range(0, D, 512)):
        cols = slice(col, col + 512)
        upd_ref[:, cols] = jnp.dot(
            att_ref[...], wo_ref[:, cols], preferred_element_type=jnp.float32
        ).astype(jnp.bfloat16)
        some = pl.ds(col, 512)
        copies.append(
            pltpu.make_async_copy(upd_ref.at[:, some], out_ref.at[finish, :, some], sems.at[4 + i])
        )
        copies[-1].start()
    for copy in copies:
        copy.wait()


def attend(xs, ats, wk, wv, held, queries, lists, finish=None, parts=(), w_out=None, earlier=()):
    n = len(xs)
    held_shape = pltpu.VMEM((4 * ROWS, D), jnp.bfloat16)
    args = [*xs, wk, wv, queries, *lists, *held]
    in_specs = [VMEM] * (n + 3) + [ANY] * 3 + [VMEM] * 2
    out_shape, out_specs = [held_shape] * 2, [VMEM] * 2
    aliases = {n + 6: 0, n + 7: 1}
    scratch = [pltpu.SMEM(x.shape, jnp.int32) for x in lists] + [pltpu.SemaphoreType.DMA((6,))]
    if finish is None:
        out_shape += [jax.ShapeDtypeStruct((2, TOK, D), jnp.float32)] * 3
        out_specs += [VMEM] * 3
    else:
        args += [*parts, in_hbm(w_out), *earlier]
        in_specs += [VMEM] * 3 + [ANY] * (1 + len(earlier))
        out_shape.append(jax.ShapeDtypeStruct((2, TOK, D), jnp.bfloat16))
        out_specs.append(ANY)
        if earlier:
            aliases[len(args) - 1] = 2
        scratch += [pltpu.VMEM((D, D), jnp.bfloat16)] + [pltpu.VMEM((TOK, D), jnp.bfloat16)] * 2
    return pl.pallas_call(
        functools.partial(attend_kernel, ats, finish),
        out_shape=out_shape,
        in_specs=in_specs,
        out_specs=out_specs,
        scratch_shapes=scratch,
        input_output_aliases=aliases,
        compiler_params=params(16 << 20),
        cost_estimate=cost(2 * TOK * D * D + 16 * TOK * SLOTS * BT * D, 8 * D * D),
    )(*args)


def local(tokens, norm_gain, modulation, w_query, w_key, w_value, w_out, neigh_list, neigh_count, cross_list):
    tiles = lax.axis_size("tile")

    def device(f, t):
        return f * tiles + t % tiles

    cells = [(f, t) for f in range(2) for t in range(tiles)]
    partner = [(device(f, t), device(1 - f, t)) for f, t in cells]
    pair = [(device(f, t), device(f, t ^ 1)) for f, t in cells]
    onward = [(device(f, t), device(1 - f, t + 1 if t % 2 else t - 1)) for f, t in cells]

    def swap(x):
        return lax.ppermute(x, BOTH, partner)

    def cross(x):
        return lax.ppermute(x, BOTH, pair)

    def forward(x):
        return lax.ppermute(x, BOTH, onward)

    def at(source, i):
        return source * ROWS + i * CR

    lists = (neigh_list, neigh_count, cross_list)
    whole, *chunks = norm(tokens, norm_gain[None], modulation)
    s0, s1 = swap(chunks[0]), swap(chunks[1])
    across = cross(whole)
    later, (queries, *own), (wk, wv) = own_project(whole, [w_query, w_key, w_value], [chunks[2]])
    s2 = swap(later[0])
    o0 = forward(s0)
    *held, token = kv_project([s0, across], [at(1, 0), 2 * ROWS], wk, wv, own, True)
    s1 = gate(s1, token)
    o1 = forward(s1)
    *held, token = kv_project([s1], [at(1, 1)], wk, wv, held, False)
    s2 = gate(s2, token)
    o2 = forward(s2)
    *held, att, peak, total = attend([s2], [at(1, 2)], wk, wv, held, queries, lists)
    parts = att, peak, total
    *held, first = attend([o0, o1], [at(3, 0), at(3, 1)], wk, wv, held, queries, lists, 0, parts, w_out)
    return attend([o2], [at(3, 2)], wk, wv, held, queries, lists, 1, parts, w_out, [first])[2]


def solution(mesh):
    return jax.shard_map(
        local,
        mesh=mesh,
        in_specs=(
            P("frame", "tile", None),
            P(),
            P("frame", None),
            P(),
            P(),
            P(),
            P(),
            P("tile", None, None),
            P("tile", None),
            P("frame", "tile", None, None),
        ),
        out_specs=P("frame", "tile", None),
        check_vma=False,
    )
```

time: 47.3 us -> 44.4 us (0.939); the launches traced: 47.2 us -> 43.9 us
  Pallas kernels: 24.6 us -> 23.4 us
  starting transfers between devices: 19 us -> 17.9 us
  waiting for transfers between devices: 3.36 us -> 2.29 us
    pallas_call x7 -> x6, Pallas kernels: 22.8 us -> 21.6 us  [the longest x3 13.8 us: attend(): pl.pallas_call(functools.partial(attend_kernel, ats, finish), out_shape=o...]
    ppermute x3, starting transfers between devices: 16.6 us -> 15.5 us  [forward(): return lax.ppermute(x, BOTH, onward)]
    ppermute x3, waiting for transfers between devices: 1.05 us -> 0.01 us  [forward(): return lax.ppermute(x, BOTH, onward)]
  transfers between devices with their start and end apart: 7 -> 7, of which waited for: 2 -> 1; matrix products, arithmetic and copies ran while one was open for 0% -> 0% of each run, Pallas kernels for 34% -> 38%
where the time goes in v3:
time: 44.4 us; the launch traced here: 43.9 us
  Pallas kernels  23.4 us (53%)
  starting transfers between devices  17.9 us (40%)
  waiting for transfers between devices  2.29 us (5%)
    ppermute x3, starting transfers between devices, forward(): return lax.ppermute(x, BOTH, onward)  15.5 us
    pallas_call x3, Pallas kernels, attend(): pl.pallas_call(functools.partial(attend_kernel, ats, finish), out_shape=o...  13.8 us
    pallas_call x1, Pallas kernels, own_project(): pl.pallas_call(functools.partial(own_kernel, n), out_shape=[jax.ShapeDtyp...  4.6 us
    pallas_call x2, Pallas kernels, kv_project(): pl.pallas_call(functools.partial(kv_kernel, ats, own), out_shape=[shape,...  3.21 us
    ppermute x3, starting transfers between devices, swap(): return lax.ppermute(x, BOTH, partner)  2.28 us
    ppermute x3, waiting for transfers between devices, swap(): return lax.ppermute(x, BOTH, partner)  2.28 us
    pallas_call x1, Pallas kernels, norm(): pl.pallas_call(norm_kernel, out_shape=[jax.ShapeDtypeStruct((ROWS, D), jn...  1.78 us
  transfers between devices with their start and end apart: 7, of which 1 were waited for; matrix products, arithmetic and copies ran while one was open for 0% of the time, Pallas kernels for 38%

profile of v3, /device:TPU:0, one launch (start us, length us, event | category | flops | bytes accessed | tf_op | source)
XLA Modules:
  0.0 43.9 jit_solution(358556225037316506)
XLA Ops:
  0.0 1.8 %shard_map.100 = (bf16[384,1024]{1,0:T(8,128)(2,1)S(1)}, bf16[128,1024]{1,0:T(8,128)(2,1)S(1)}, bf16[128,1024]{1,0:T(8,128)(2,1)S(1)}, bf16[128,1024]{1,0:T(8,128)(2,1)S(1)}) custom-call(bf16[2,192,1024]{2,1,0:T(8,128)(2,1)} %tok_hbm.1, f32[1,1024]{1,0:T(1,128)} %bitcast.1, f32[2,1024]{1,0:T(2,128)} %mod_hbm.1), custom_call_target="tpu_custom_call" | custom-call | flops 3145728 | bytes 2359296 | tf_op jit(solution)/shard_map/pallas_call | solution.py:76
  1.8 0.1 collective-permute-start.3
  1.9 0.1 collective-permute-start.2
  2.0 2.0 %collective-permute-start.1 = (bf16[128,1024]{1,0:T(8,128)(2,1)S(1)}, bf16[128,1024]{1,0:T(8,128)(2,1)S(1)}, u32[]{:S(2)}, u32[]{:S(2)}) collective-permute-start(bf16[128,1024]{1,0:T(8,128)(2,1)S(1)} %get-tuple-element.33), channel_id=1, source_target_pairs={{0,128},{1,129},{2,130},{3,131},{4,132},{5,133},{6,134},{7,135},{8... | collective-permute-start | bytes 786440 | tf_op jit(solution)/shard_map/ppermute | solution.py:359
  4.0 0.0 copy-start.2
  4.0 0.0 copy-start.1
  4.0 4.6 %shard_map.101 = (bf16[128,1024]{1,0:T(8,128)(2,1)S(1)}, bf16[384,1024]{1,0:T(8,128)(2,1)S(1)}, bf16[384,1024]{1,0:T(8,128)(2,1)S(1)}, bf16[384,1024]{1,0:T(8,12...) custom-call(bf16[384,1024]{1,0:T(8,128)(2,1)S(1)} %get-tuple-element., ...), custom_call_target="tpu_custom_call", output_to_operand_aliasing={{0}: (4, {})} | custom-call | flops 2415919104 | bytes 6291456 | tf_op jit(solution)/shard_map/pallas_call | solution.py:116
  8.6 0.2 collective-permute-start
  8.8 0.0 copy-done.2
  8.8 0.0 copy-done.1
  8.8 2.3 %collective-permute-done.2.refs_0_ = bf16[128,1024]{1,0:T(8,128)(2,1)S(1)} collective-permute-done((bf16[128,1024]{1,0:T(8,128)(2,1)S(1)}, bf16[128,1024]{1,0:T(8,128)(2,1)S(1)}, u32[]{:S(2)}, u32[]{:S(2)}) %collective-permute-start.2) | collective-permute-done | bytes 262176 | tf_op jit(solution)/shard_map/ppermute | solution.py:359
  11.1 7.5 %collective-permute-start.5 = (bf16[128,1024]{1,0:T(8,128)(2,1)S(1)}, bf16[128,1024]{1,0:T(8,128)(2,1)S(1)}, u32[]{:S(2)}, u32[]{:S(2)}) collective-permute-start(bf16[128,1024]{1,0:T(8,128)(2,1)S(1)} %collective-permute-done.2.refs_0_), channel_id=1, source_target_pairs={{0,255},{1,130},{2,129},{3,132},{4,131},{5,134},{6,133},{7,136},{8... | collective-permute-start | bytes 786440 | tf_op jit(solution)/shard_map/ppermute | solution.py:365
  18.6 0.0 collective-permute-done.3.refs_1_
  18.6 2.5 %shard_map.102 = (bf16[1536,1024]{1,0:T(8,128)(2,1)S(1)}, bf16[1536,1024]{1,0:T(8,128)(2,1)S(1)}, f32[8,128]{1,0:T(8,128)S(1)}) custom-call(bf16[128,1024]{1,0:T(8,128)(2,1)S(1)} %collective-permute-done.2.refs_0_, bf16[384,1024]{1,0:T(8,128)(2,1)S(1)} %collective-permute-done.3.refs_1_, bf16[1024,1024]{1,0:T(8,128)(2,1)S(1)} %get-tuple-element.35.refs_2_.refs_1_, ...), custom_call_target="tpu_custom_call" | custom-call | flops 2147483648 | bytes 6291456 | tf_op jit(solution)/shard_map/pallas_call | solution.py:177
  21.1 0.0 collective-permute-done.1.refs_0_
  21.1 3.1 %collective-permute-start.6 = (bf16[128,1024]{1,0:T(8,128)(2,1)S(1)}, bf16[128,1024]{1,0:T(8,128)(2,1)S(1)}, u32[]{:S(2)}, u32[]{:S(2)}) collective-permute-start(bf16[128,1024]{1,0:T(8,128)(2,1)S(1)} %shard_map.103.refs_0_), channel_id=1, source_target_pairs={{0,255},{1,130},{2,129},{3,132},{4,131},{5,134},{6,133},{7,136},{8... | collective-permute-start | bytes 786440 | tf_op jit(solution)/shard_map/ppermute | solution.py:365
  24.2 0.0 copy-start
  24.2 0.7 %shard_map.104 = (bf16[1536,1024]{1,0:T(8,128)(2,1)S(1)}, bf16[1536,1024]{1,0:T(8,128)(2,1)S(1)}, f32[8,128]{1,0:T(8,128)S(1)}) custom-call(bf16[128,1024]{1,0:T(8,128)(2,1)S(1)} %shard_map.103.refs_0_, bf16[1024,1024]{1,0:T(8,128)(2,1)S(1)} %get-tuple-element.35.refs_2_.refs_1_, ...), custom_call_target="tpu_custom_call", output_to_operand_aliasing={{0}: (3, {}), {1}: (4, {})} | custom-call | flops 536870912 | bytes 6291456 | tf_op jit(solution)/shard_map/pallas_call | solution.py:177
  25.0 0.0 collective-permute-done.refs_0_
  25.0 4.9 %collective-permute-start.4 = (bf16[128,1024]{1,0:T(8,128)(2,1)S(1)}, bf16[128,1024]{1,0:T(8,128)(2,1)S(1)}, u32[]{:S(2)}, u32[]{:S(2)}) collective-permute-start(bf16[128,1024]{1,0:T(8,128)(2,1)S(1)} %shard_map.105.refs_0_), channel_id=1, source_target_pairs={{0,255},{1,130},{2,129},{3,132},{4,131},{5,134},{6,133},{7,136},{8... | collective-permute-start | bytes 786440 | tf_op jit(solution)/shard_map/ppermute | solution.py:365
  29.9 0.0 copy-done
  29.9 3.3 %shard_map.106 = (bf16[1536,1024]{1,0:T(8,128)(2,1)S(1)}, bf16[1536,1024]{1,0:T(8,128)(2,1)S(1)}, f32[2,192,1024]{2,1,0:T(8,128)S(1)}, f32[2,192,1024]{2,1,0:T(8,128)S(1)}, f32[2,192,1024]{2,1,0:T(8,128)S(1)}) custom-call(bf16[128,1024]{1,0:T(8,128)(2,1)S(1)} %shard_map.105.refs_0_, ...), custom_call_target="tpu_custom_call", output_to_operand_aliasing={{0}: (7, {}), {1}: (8, {})} | custom-call | flops 2415919104 | bytes 8388608 | tf_op jit(solution)/shard_map/pallas_call | solution.py:335
  33.1 0.0 collective-permute-done.5.refs_0_
  33.1 0.0 collective-permute-done.6.refs_1_
  33.2 5.4 %shard_map.107 = (bf16[1536,1024]{1,0:T(8,128)(2,1)S(1)}, bf16[1536,1024]{1,0:T(8,128)(2,1)S(1)}, bf16[2,192,1024]{2,1,0:T(8,128)(2,1)}) custom-call(bf16[128,1024]{1,0:T(8,128)(2,1)S(1)} %collective-permute-done.5.refs_0_, bf16[128,1024]{1,0:T(8,128)(2,1)S(1)} %collective-permute-done.6.refs_1_, ...), custom_call_target="tpu_custom_call", output_to_operand_aliasing={{0}: (8, {}), {1}: (9, {})} | custom-call | flops 2415919104 | bytes 8388608 | tf_op jit(solution)/shard_map/pallas_call | solution.py:335
  38.6 0.0 collective-permute-done.4.refs_0_
  38.6 5.1 %shard_map.108 = (bf16[1536,1024]{1,0:T(8,128)(2,1)S(1)}, bf16[1536,1024]{1,0:T(8,128)(2,1)S(1)}, bf16[2,192,1024]{2,1,0:T(8,128)(2,1)}) custom-call(bf16[128,1024]{1,0:T(8,128)(2,1)S(1)} %collective-permute-done.4.refs_0_, bf16[1024,1024]{1,0:T(8,128)(2,1)S(1)} %get-tuple-element.35.refs_2_.refs_1_, ...), custom_call_target="tpu_custom_call", output_to_operand_aliasing={{0}: (7, {}), {1}: (8, {}), {2}: (13, {})} | custom-call | flops 2415919104 | bytes 8388608 | tf_op jit(solution)/shard_map/pallas_call | solution.py:335
  (4 shorter events, 0.0 us)
Async XLA Ops:
  1.8 16.8 %collective-permute-start.3 = (bf16[384,1024]{1,0:T(8,128)(2,1)S(1)}, bf16[384,1024]{1,0:T(8,128)(2,1)S(1)}, u32[]{:S(2)}, u32[]{:S(2)}) collective-permute-start(bf16[384,1024]{1,0:T(8,128)(2,1)S(1)} %get-tuple-element.30.refs_0_), channel_id=1, source_target_pairs={{0,1},{1,0},{2,3},{3,2},{4,5},{5,4},{6,7},{7,6},{8,9},{9,8},{10,11... | collective-permute-start | bytes 2359304 | tf_op jit(solution)/shard_map/ppermute | solution.py:362
  1.9 9.2 %collective-permute-start.2 = (bf16[128,1024]{1,0:T(8,128)(2,1)S(1)}, bf16[128,1024]{1,0:T(8,128)(2,1)S(1)}, u32[]{:S(2)}, u32[]{:S(2)}) collective-permute-start(bf16[128,1024]{1,0:T(8,128)(2,1)S(1)} %get-tuple-element.34), channel_id=1, source_target_pairs={{0,128},{1,129},{2,130},{3,131},{4,132},{5,133},{6,134},{7,135},{8... | collective-permute-start | bytes 786440 | tf_op jit(solution)/shard_map/ppermute | solution.py:359
  2.0 19.1 %collective-permute-start.1 = (bf16[128,1024]{1,0:T(8,128)(2,1)S(1)}, bf16[128,1024]{1,0:T(8,128)(2,1)S(1)}, u32[]{:S(2)}, u32[]{:S(2)}) collective-permute-start(bf16[128,1024]{1,0:T(8,128)(2,1)S(1)} %get-tuple-element.33), channel_id=1, source_target_pairs={{0,128},{1,129},{2,130},{3,131},{4,132},{5,133},{6,134},{7,135},{8... | collective-permute-start | bytes 786440 | tf_op jit(solution)/shard_map/ppermute | solution.py:359
  4.0 4.8 %copy-start.2 = (s32[1,3,6]{2,0,1:T(1,128)S(1)}, s32[1,3,6]{2,0,1:T(1,128)}, u32[]{:S(2)}) copy-start(s32[1,3,6]{2,0,1:T(1,128)} %param.17) | copy-start | bytes 220
  4.0 4.8 %copy-start.1 = (s32[2,1,3,4]{3,1,2,0:T(1,128)S(1)}, s32[2,1,3,4]{3,1,2,0:T(1,128)}, u32[]{:S(2)}) copy-start(s32[2,1,3,4]{3,1,2,0:T(1,128)} %param.19) | copy-start | bytes 292
  8.6 16.4 %collective-permute-start = (bf16[128,1024]{1,0:T(8,128)(2,1)S(1)}, bf16[128,1024]{1,0:T(8,128)(2,1)S(1)}, u32[]{:S(2)}, u32[]{:S(2)}) collective-permute-start(bf16[128,1024]{1,0:T(8,128)(2,1)S(1)} %get-tuple-element.32), channel_id=1, source_target_pairs={{0,128},{1,129},{2,130},{3,131},{4,132},{5,133},{6,134},{7,135},{8... | collective-permute-start | bytes 786440 | tf_op jit(solution)/shard_map/ppermute | solution.py:359
  11.1 22.0 %collective-permute-start.5 = (bf16[128,1024]{1,0:T(8,128)(2,1)S(1)}, bf16[128,1024]{1,0:T(8,128)(2,1)S(1)}, u32[]{:S(2)}, u32[]{:S(2)}) collective-permute-start(bf16[128,1024]{1,0:T(8,128)(2,1)S(1)} %collective-permute-done.2.refs_0_), channel_id=1, source_target_pairs={{0,255},{1,130},{2,129},{3,132},{4,131},{5,134},{6,133},{7,136},{8... | collective-permute-start | bytes 786440 | tf_op jit(solution)/shard_map/ppermute | solution.py:365
  21.1 12.0 %collective-permute-start.6 = (bf16[128,1024]{1,0:T(8,128)(2,1)S(1)}, bf16[128,1024]{1,0:T(8,128)(2,1)S(1)}, u32[]{:S(2)}, u32[]{:S(2)}) collective-permute-start(bf16[128,1024]{1,0:T(8,128)(2,1)S(1)} %shard_map.103.refs_0_), channel_id=1, source_target_pairs={{0,255},{1,130},{2,129},{3,132},{4,131},{5,134},{6,133},{7,136},{8... | collective-permute-start | bytes 786440 | tf_op jit(solution)/shard_map/ppermute | solution.py:365
  24.2 5.6 %copy-start = (s32[1,3]{1,0:T(1,128)S(1)}, s32[1,3]{1,0:T(1,128)}, u32[]{:S(2)}) copy-start(s32[1,3]{1,0:T(1,128)} %refs_5_.4) | copy-start | bytes 40
  25.0 13.6 %collective-permute-start.4 = (bf16[128,1024]{1,0:T(8,128)(2,1)S(1)}, bf16[128,1024]{1,0:T(8,128)(2,1)S(1)}, u32[]{:S(2)}, u32[]{:S(2)}) collective-permute-start(bf16[128,1024]{1,0:T(8,128)(2,1)S(1)} %shard_map.105.refs_0_), channel_id=1, source_target_pairs={{0,255},{1,130},{2,129},{3,132},{4,131},{5,134},{6,133},{7,136},{8... | collective-permute-start | bytes 786440 | tf_op jit(solution)/shard_map/ppermute | solution.py:365

commit v4 on v3

--- a/solution.py
+++ b/solution.py
@@ -27,6 +27,7 @@
 BOTH = ("frame", "tile")
 VMEM = pl.BlockSpec(memory_space=pltpu.VMEM)
 ANY = pl.BlockSpec(memory_space=pl.ANY)
+FAR_AHEAD = 64.0
 EXP_SCALE = float(np.log2(np.e) / np.sqrt(HEAD))
 
 
@@ -198,16 +199,19 @@
     wk_ref, wv_ref, q_ref, neigh_hbm, count_hbm, cross_hbm = take(6)
     take(2)
     if finish is not None:
-        part_refs, (wo_hbm,) = take(3), take(1)
-        take(finish)
+        part_refs, (wo_hbm,) = take(2), take(1)
+    if finish == 1:
+        (first_ref,) = take(1)
     k_ref, v_ref = take(2)
     if finish is None:
-        part_refs = take(3)
+        part_refs = take(2)
     else:
         (out_ref,) = take(1)
     neigh_ref, count_ref, cross_ref, sems = take(4)
     if finish is not None:
-        wo_ref, att_ref, upd_ref = take(3)
+        wo_ref, att_ref = take(2)
+    if finish == 1:
+        (upd_ref,) = take(1)
     lists = [
         pltpu.make_async_copy(neigh_hbm, neigh_ref, sems.at[0]),
         pltpu.make_async_copy(count_hbm, count_ref, sems.at[1]),
@@ -218,6 +222,10 @@
     if finish is not None:
         wo_copy = pltpu.make_async_copy(wo_hbm, wo_ref, sems.at[3])
         wo_copy.start()
+    copies = []
+    if finish == 1:
+        copies.append(pltpu.make_async_copy(first_ref, out_ref.at[0], sems.at[4]))
+        copies[0].start()
     project_rows(x_refs, ats, ((wk_ref, k_ref), (wv_ref, v_ref)))
     for copy in lists:
         copy.wait()
@@ -288,50 +296,55 @@
     if finish is None:
         for frame in range(2):
             for where, values in parts(frame, far_slots, False):
-                for ref, value in zip(part_refs, values):
-                    ref[(frame, *where)] = value
+                att, peak, total = values
+                part_refs[0][(frame, *where)] = att / total
+                part_refs[1][(frame, *where)] = peak * EXP_SCALE + jnp.log2(total)
         return
     for where, (att, peak, total) in parts(finish, near_slots, True):
-        att2, peak2, total2 = (ref[(finish, *where)] for ref in part_refs)
-        top = jnp.maximum(peak, peak2)
-        scale, scale2 = jnp.exp2((peak - top) * EXP_SCALE), jnp.exp2((peak2 - top) * EXP_SCALE)
-        whole = total * scale + total2 * scale2
-        att_ref[where] = ((att * scale + att2 * scale2) / whole).astype(jnp.bfloat16)
+        far, level = (ref[(finish, *where)] for ref in part_refs)
+        scale = jnp.exp2(jnp.minimum(peak * EXP_SCALE - level, FAR_AHEAD))
+        att_ref[where] = ((far + att * scale) / (1.0 + total * scale)).astype(jnp.bfloat16)
     wo_copy.wait()
-    copies = []
-    for i, col in enumerate(range(0, D, 512)):
-        cols = slice(col, col + 512)
+    if finish == 0:
+        project_into(att_ref[...], wo_ref, out_ref, 0)
+        return
+    for i, col in enumerate(range(0, D, 256)):
+        cols = slice(col, col + 256)
         upd_ref[:, cols] = jnp.dot(
             att_ref[...], wo_ref[:, cols], preferred_element_type=jnp.float32
         ).astype(jnp.bfloat16)
-        some = pl.ds(col, 512)
-        copies.append(
-            pltpu.make_async_copy(upd_ref.at[:, some], out_ref.at[finish, :, some], sems.at[4 + i])
-        )
+        some = pl.ds(col, 256)
+        copies.append(pltpu.make_async_copy(upd_ref.at[:, some], out_ref.at[1, :, some], sems.at[5 + i]))
         copies[-1].start()
     for copy in copies:
         copy.wait()
 
 
-def attend(xs, ats, wk, wv, held, queries, lists, finish=None, parts=(), w_out=None, earlier=()):
+def attend(xs, ats, wk, wv, held, queries, lists, finish=None, parts=(), w_out=None, first=None):
     n = len(xs)
     held_shape = pltpu.VMEM((4 * ROWS, D), jnp.bfloat16)
     args = [*xs, wk, wv, queries, *lists, *held]
     in_specs = [VMEM] * (n + 3) + [ANY] * 3 + [VMEM] * 2
     out_shape, out_specs = [held_shape] * 2, [VMEM] * 2
     aliases = {n + 6: 0, n + 7: 1}
-    scratch = [pltpu.SMEM(x.shape, jnp.int32) for x in lists] + [pltpu.SemaphoreType.DMA((6,))]
+    scratch = [pltpu.SMEM(x.shape, jnp.int32) for x in lists] + [pltpu.SemaphoreType.DMA((9,))]
+    rows = pltpu.VMEM((TOK, D), jnp.bfloat16)
     if finish is None:
-        out_shape += [jax.ShapeDtypeStruct((2, TOK, D), jnp.float32)] * 3
-        out_specs += [VMEM] * 3
+        out_shape += [jax.ShapeDtypeStruct((2, TOK, D), jnp.float32)] * 2
+        out_specs += [VMEM] * 2
     else:
-        args += [*parts, in_hbm(w_out), *earlier]
-        in_specs += [VMEM] * 3 + [ANY] * (1 + len(earlier))
+        args += [*parts, in_hbm(w_out)]
+        in_specs += [VMEM] * 2 + [ANY]
+        scratch += [pltpu.VMEM((D, D), jnp.bfloat16), rows]
+    if finish == 0:
+        out_shape.append(rows)
+        out_specs.append(VMEM)
+    if finish == 1:
+        args.append(first)
+        in_specs.append(VMEM)
         out_shape.append(jax.ShapeDtypeStruct((2, TOK, D), jnp.bfloat16))
         out_specs.append(ANY)
-        if earlier:
-            aliases[len(args) - 1] = 2
-        scratch += [pltpu.VMEM((D, D), jnp.bfloat16)] + [pltpu.VMEM((TOK, D), jnp.bfloat16)] * 2
+        scratch.append(rows)
     return pl.pallas_call(
         functools.partial(attend_kernel, ats, finish),
         out_shape=out_shape,
@@ -380,10 +393,10 @@
     *held, token = kv_project([s1], [at(1, 1)], wk, wv, held, False)
     s2 = gate(s2, token)
     o2 = forward(s2)
-    *held, att, peak, total = attend([s2], [at(1, 2)], wk, wv, held, queries, lists)
-    parts = att, peak, total
+    *held, far, level = attend([s2], [at(1, 2)], wk, wv, held, queries, lists)
+    parts = far, level
     *held, first = attend([o0, o1], [at(3, 0), at(3, 1)], wk, wv, held, queries, lists, 0, parts, w_out)
-    return attend([o2], [at(3, 2)], wk, wv, held, queries, lists, 1, parts, w_out, [first])[2]
+    return attend([o2], [at(3, 2)], wk, wv, held, queries, lists, 1, parts, w_out, first)[2]
 
 
 def solution(mesh):

time: 44.4 us -> 43.7 us (0.984)
  Pallas kernels: 23.4 us -> 22.7 us
    pallas_call x3, Pallas kernels: 13.8 us -> 13.1 us  [attend(): pl.pallas_call(functools.partial(attend_kernel, ats, finish), out_shape=o...]
  transfers between devices with their start and end apart: 7 -> 7, of which waited for: 1 -> 1; matrix products, arithmetic and copies ran while one was open for 0% -> 0% of each run, Pallas kernels for 38% -> 37%
where the time goes in v4:
time: 43.7 us; the launch traced here: 43.1 us
  Pallas kernels  22.7 us (52%)
  starting transfers between devices  17.9 us (41%)
  waiting for transfers between devices  2.29 us (5%)
    ppermute x3, starting transfers between devices, forward(): return lax.ppermute(x, BOTH, onward)  15.5 us
    pallas_call x3, Pallas kernels, attend(): pl.pallas_call(functools.partial(attend_kernel, ats, finish), out_shape=o...  13.1 us
    pallas_call x1, Pallas kernels, own_project(): pl.pallas_call(functools.partial(own_kernel, n), out_shape=[jax.ShapeDtyp...  4.6 us
    pallas_call x2, Pallas kernels, kv_project(): pl.pallas_call(functools.partial(kv_kernel, ats, own), out_shape=[shape,...  3.21 us
    ppermute x3, starting transfers between devices, swap(): return lax.ppermute(x, BOTH, partner)  2.28 us
    ppermute x3, waiting for transfers between devices, swap(): return lax.ppermute(x, BOTH, partner)  2.28 us
    pallas_call x1, Pallas kernels, norm(): pl.pallas_call(norm_kernel, out_shape=[jax.ShapeDtypeStruct((ROWS, D), jn...  1.78 us
  transfers between devices with their start and end apart: 7, of which 1 were waited for; matrix products, arithmetic and copies ran while one was open for 0% of the time, Pallas kernels for 37%

profile of v4, /device:TPU:0, one launch (start us, length us, event | category | flops | bytes accessed | tf_op | source)
XLA Modules:
  0.0 43.1 jit_solution(7111154145755901414)
XLA Ops:
  0.0 1.8 %shard_map.100 = (bf16[384,1024]{1,0:T(8,128)(2,1)S(1)}, bf16[128,1024]{1,0:T(8,128)(2,1)S(1)}, bf16[128,1024]{1,0:T(8,128)(2,1)S(1)}, bf16[128,1024]{1,0:T(8,128)(2,1)S(1)}) custom-call(bf16[2,192,1024]{2,1,0:T(8,128)(2,1)} %tok_hbm.1, f32[1,1024]{1,0:T(1,128)} %bitcast.1, f32[2,1024]{1,0:T(2,128)} %mod_hbm.1), custom_call_target="tpu_custom_call" | custom-call | flops 3145728 | bytes 2359296 | tf_op jit(solution)/shard_map/pallas_call | solution.py:77
  1.8 0.1 collective-permute-start.3
  1.9 0.1 collective-permute-start.2
  2.0 2.0 %collective-permute-start.1 = (bf16[128,1024]{1,0:T(8,128)(2,1)S(1)}, bf16[128,1024]{1,0:T(8,128)(2,1)S(1)}, u32[]{:S(2)}, u32[]{:S(2)}) collective-permute-start(bf16[128,1024]{1,0:T(8,128)(2,1)S(1)} %get-tuple-element.32), channel_id=1, source_target_pairs={{0,128},{1,129},{2,130},{3,131},{4,132},{5,133},{6,134},{7,135},{8... | collective-permute-start | bytes 786440 | tf_op jit(solution)/shard_map/ppermute | solution.py:372
  4.0 0.0 copy-start.2
  4.0 0.0 copy-start.1
  4.0 4.6 %shard_map.101 = (bf16[128,1024]{1,0:T(8,128)(2,1)S(1)}, bf16[384,1024]{1,0:T(8,128)(2,1)S(1)}, bf16[384,1024]{1,0:T(8,128)(2,1)S(1)}, bf16[384,1024]{1,0:T(8,12...) custom-call(bf16[384,1024]{1,0:T(8,128)(2,1)S(1)} %get-tuple-element., ...), custom_call_target="tpu_custom_call", output_to_operand_aliasing={{0}: (4, {})} | custom-call | flops 2415919104 | bytes 6291456 | tf_op jit(solution)/shard_map/pallas_call | solution.py:117
  8.6 0.2 collective-permute-start
  8.8 0.0 copy-done.2
  8.8 0.0 copy-done.1
  8.8 2.3 %collective-permute-done.2.refs_0_ = bf16[128,1024]{1,0:T(8,128)(2,1)S(1)} collective-permute-done((bf16[128,1024]{1,0:T(8,128)(2,1)S(1)}, bf16[128,1024]{1,0:T(8,128)(2,1)S(1)}, u32[]{:S(2)}, u32[]{:S(2)}) %collective-permute-start.2) | collective-permute-done | bytes 262176 | tf_op jit(solution)/shard_map/ppermute | solution.py:372
  11.1 7.5 %collective-permute-start.5 = (bf16[128,1024]{1,0:T(8,128)(2,1)S(1)}, bf16[128,1024]{1,0:T(8,128)(2,1)S(1)}, u32[]{:S(2)}, u32[]{:S(2)}) collective-permute-start(bf16[128,1024]{1,0:T(8,128)(2,1)S(1)} %collective-permute-done.2.refs_0_), channel_id=1, source_target_pairs={{0,255},{1,130},{2,129},{3,132},{4,131},{5,134},{6,133},{7,136},{8... | collective-permute-start | bytes 786440 | tf_op jit(solution)/shard_map/ppermute | solution.py:378
  18.6 0.0 collective-permute-done.3.refs_1_
  18.6 2.5 %shard_map.102 = (bf16[1536,1024]{1,0:T(8,128)(2,1)S(1)}, bf16[1536,1024]{1,0:T(8,128)(2,1)S(1)}, f32[8,128]{1,0:T(8,128)S(1)}) custom-call(bf16[128,1024]{1,0:T(8,128)(2,1)S(1)} %collective-permute-done.2.refs_0_, bf16[384,1024]{1,0:T(8,128)(2,1)S(1)} %collective-permute-done.3.refs_1_, bf16[1024,1024]{1,0:T(8,128)(2,1)S(1)} %get-tuple-element.34.refs_2_.refs_1_, ...), custom_call_target="tpu_custom_call" | custom-call | flops 2147483648 | bytes 6291456 | tf_op jit(solution)/shard_map/pallas_call | solution.py:178
  21.1 0.0 collective-permute-done.1.refs_0_
  21.1 3.1 %collective-permute-start.6 = (bf16[128,1024]{1,0:T(8,128)(2,1)S(1)}, bf16[128,1024]{1,0:T(8,128)(2,1)S(1)}, u32[]{:S(2)}, u32[]{:S(2)}) collective-permute-start(bf16[128,1024]{1,0:T(8,128)(2,1)S(1)} %shard_map.103.refs_0_), channel_id=1, source_target_pairs={{0,255},{1,130},{2,129},{3,132},{4,131},{5,134},{6,133},{7,136},{8... | collective-permute-start | bytes 786440 | tf_op jit(solution)/shard_map/ppermute | solution.py:378
  24.2 0.0 copy-start
  24.2 0.7 %shard_map.104 = (bf16[1536,1024]{1,0:T(8,128)(2,1)S(1)}, bf16[1536,1024]{1,0:T(8,128)(2,1)S(1)}, f32[8,128]{1,0:T(8,128)S(1)}) custom-call(bf16[128,1024]{1,0:T(8,128)(2,1)S(1)} %shard_map.103.refs_0_, bf16[1024,1024]{1,0:T(8,128)(2,1)S(1)} %get-tuple-element.34.refs_2_.refs_1_, ...), custom_call_target="tpu_custom_call", output_to_operand_aliasing={{0}: (3, {}), {1}: (4, {})} | custom-call | flops 536870912 | bytes 6291456 | tf_op jit(solution)/shard_map/pallas_call | solution.py:178
  25.0 0.0 collective-permute-done.refs_0_
  25.0 4.9 %collective-permute-start.4 = (bf16[128,1024]{1,0:T(8,128)(2,1)S(1)}, bf16[128,1024]{1,0:T(8,128)(2,1)S(1)}, u32[]{:S(2)}, u32[]{:S(2)}) collective-permute-start(bf16[128,1024]{1,0:T(8,128)(2,1)S(1)} %shard_map.105.refs_0_), channel_id=1, source_target_pairs={{0,255},{1,130},{2,129},{3,132},{4,131},{5,134},{6,133},{7,136},{8... | collective-permute-start | bytes 786440 | tf_op jit(solution)/shard_map/ppermute | solution.py:378
  29.9 0.0 copy-done
  29.9 3.5 %shard_map.106 = (bf16[1536,1024]{1,0:T(8,128)(2,1)S(1)}, bf16[1536,1024]{1,0:T(8,128)(2,1)S(1)}, f32[2,192,1024]{2,1,0:T(8,128)S(1)}, f32[2,192,1024]{2,1,0:T(8,128)S(1)}) custom-call(bf16[128,1024]{1,0:T(8,128)(2,1)S(1)} %shard_map.105.refs_0_, ...), custom_call_target="tpu_custom_call", output_to_operand_aliasing={{0}: (7, {}), {1}: (8, {})} | custom-call | flops 2415919104 | bytes 8388608 | tf_op jit(solution)/shard_map/pallas_call | solution.py:348
  33.4 0.0 collective-permute-done.5.refs_0_
  33.4 0.0 collective-permute-done.6.refs_1_
  33.4 4.6 %shard_map.107 = (bf16[1536,1024]{1,0:T(8,128)(2,1)S(1)}, bf16[1536,1024]{1,0:T(8,128)(2,1)S(1)}, bf16[192,1024]{1,0:T(8,128)(2,1)S(1)}) custom-call(bf16[128,1024]{1,0:T(8,128)(2,1)S(1)} %collective-permute-done.5.refs_0_, bf16[128,1024]{1,0:T(8,128)(2,1)S(1)} %collective-permute-done.6.refs_1_, ...), custom_call_target="tpu_custom_call", output_to_operand_aliasing={{0}: (8, {}), {1}: (9, {})} | custom-call | flops 2415919104 | bytes 8388608 | tf_op jit(solution)/shard_map/pallas_call | solution.py:348
  38.0 0.0 collective-permute-done.4.refs_0_
  38.0 4.9 %shard_map.108 = (bf16[1536,1024]{1,0:T(8,128)(2,1)S(1)}, bf16[1536,1024]{1,0:T(8,128)(2,1)S(1)}, bf16[2,192,1024]{2,1,0:T(8,128)(2,1)}) custom-call(bf16[128,1024]{1,0:T(8,128)(2,1)S(1)} %collective-permute-done.4.refs_0_, bf16[1024,1024]{1,0:T(8,128)(2,1)S(1)} %get-tuple-element.34.refs_2_.refs_1_, ...), custom_call_target="tpu_custom_call", output_to_operand_aliasing={{0}: (7, {}), {1}: (8, {})} | custom-call | flops 2415919104 | bytes 8388608 | tf_op jit(solution)/shard_map/pallas_call | solution.py:348
  (4 shorter events, 0.0 us)
Async XLA Ops:
  1.8 16.8 %collective-permute-start.3 = (bf16[384,1024]{1,0:T(8,128)(2,1)S(1)}, bf16[384,1024]{1,0:T(8,128)(2,1)S(1)}, u32[]{:S(2)}, u32[]{:S(2)}) collective-permute-start(bf16[384,1024]{1,0:T(8,128)(2,1)S(1)} %get-tuple-element.29.refs_0_), channel_id=1, source_target_pairs={{0,1},{1,0},{2,3},{3,2},{4,5},{5,4},{6,7},{7,6},{8,9},{9,8},{10,11... | collective-permute-start | bytes 2359304 | tf_op jit(solution)/shard_map/ppermute | solution.py:375
  1.9 9.2 %collective-permute-start.2 = (bf16[128,1024]{1,0:T(8,128)(2,1)S(1)}, bf16[128,1024]{1,0:T(8,128)(2,1)S(1)}, u32[]{:S(2)}, u32[]{:S(2)}) collective-permute-start(bf16[128,1024]{1,0:T(8,128)(2,1)S(1)} %get-tuple-element.33), channel_id=1, source_target_pairs={{0,128},{1,129},{2,130},{3,131},{4,132},{5,133},{6,134},{7,135},{8... | collective-permute-start | bytes 786440 | tf_op jit(solution)/shard_map/ppermute | solution.py:372
  2.0 19.1 %collective-permute-start.1 = (bf16[128,1024]{1,0:T(8,128)(2,1)S(1)}, bf16[128,1024]{1,0:T(8,128)(2,1)S(1)}, u32[]{:S(2)}, u32[]{:S(2)}) collective-permute-start(bf16[128,1024]{1,0:T(8,128)(2,1)S(1)} %get-tuple-element.32), channel_id=1, source_target_pairs={{0,128},{1,129},{2,130},{3,131},{4,132},{5,133},{6,134},{7,135},{8... | collective-permute-start | bytes 786440 | tf_op jit(solution)/shard_map/ppermute | solution.py:372
  4.0 4.8 %copy-start.2 = (s32[1,3,6]{2,0,1:T(1,128)S(1)}, s32[1,3,6]{2,0,1:T(1,128)}, u32[]{:S(2)}) copy-start(s32[1,3,6]{2,0,1:T(1,128)} %param.17) | copy-start | bytes 220
  4.0 4.8 %copy-start.1 = (s32[2,1,3,4]{3,1,2,0:T(1,128)S(1)}, s32[2,1,3,4]{3,1,2,0:T(1,128)}, u32[]{:S(2)}) copy-start(s32[2,1,3,4]{3,1,2,0:T(1,128)} %param.19) | copy-start | bytes 292
  8.6 16.4 %collective-permute-start = (bf16[128,1024]{1,0:T(8,128)(2,1)S(1)}, bf16[128,1024]{1,0:T(8,128)(2,1)S(1)}, u32[]{:S(2)}, u32[]{:S(2)}) collective-permute-start(bf16[128,1024]{1,0:T(8,128)(2,1)S(1)} %get-tuple-element.31), channel_id=1, source_target_pairs={{0,128},{1,129},{2,130},{3,131},{4,132},{5,133},{6,134},{7,135},{8... | collective-permute-start | bytes 786440 | tf_op jit(solution)/shard_map/ppermute | solution.py:372
  11.1 22.3 %collective-permute-start.5 = (bf16[128,1024]{1,0:T(8,128)(2,1)S(1)}, bf16[128,1024]{1,0:T(8,128)(2,1)S(1)}, u32[]{:S(2)}, u32[]{:S(2)}) collective-permute-start(bf16[128,1024]{1,0:T(8,128)(2,1)S(1)} %collective-permute-done.2.refs_0_), channel_id=1, source_target_pairs={{0,255},{1,130},{2,129},{3,132},{4,131},{5,134},{6,133},{7,136},{8... | collective-permute-start | bytes 786440 | tf_op jit(solution)/shard_map/ppermute | solution.py:378
  21.1 12.3 %collective-permute-start.6 = (bf16[128,1024]{1,0:T(8,128)(2,1)S(1)}, bf16[128,1024]{1,0:T(8,128)(2,1)S(1)}, u32[]{:S(2)}, u32[]{:S(2)}) collective-permute-start(bf16[128,1024]{1,0:T(8,128)(2,1)S(1)} %shard_map.103.refs_0_), channel_id=1, source_target_pairs={{0,255},{1,130},{2,129},{3,132},{4,131},{5,134},{6,133},{7,136},{8... | collective-permute-start | bytes 786440 | tf_op jit(solution)/shard_map/ppermute | solution.py:378
  24.2 5.6 %copy-start = (s32[1,3]{1,0:T(1,128)S(1)}, s32[1,3]{1,0:T(1,128)}, u32[]{:S(2)}) copy-start(s32[1,3]{1,0:T(1,128)} %refs_5_.4) | copy-start | bytes 40
  25.0 13.0 %collective-permute-start.4 = (bf16[128,1024]{1,0:T(8,128)(2,1)S(1)}, bf16[128,1024]{1,0:T(8,128)(2,1)S(1)}, u32[]{:S(2)}, u32[]{:S(2)}) collective-permute-start(bf16[128,1024]{1,0:T(8,128)(2,1)S(1)} %shard_map.105.refs_0_), channel_id=1, source_target_pairs={{0,255},{1,130},{2,129},{3,132},{4,131},{5,134},{6,133},{7,136},{8... | collective-permute-start | bytes 786440 | tf_op jit(solution)/shard_map/ppermute | solution.py:378

commit v5 on v4

--- a/solution.py
+++ b/solution.py
@@ -46,23 +46,18 @@
 def norm_kernel(tok_hbm, gain_hbm, mod_hbm, whole_ref, *rest):
     chunk_refs, (tok_ref, gain_ref, mod_ref, sems) = rest[:CHUNKS], rest[CHUNKS:]
     side = [
-        pltpu.make_async_copy(gain_hbm, gain_ref, sems.at[ROWS // STEP]),
-        pltpu.make_async_copy(mod_hbm, mod_ref, sems.at[ROWS // STEP + 1]),
+        pltpu.make_async_copy(gain_hbm, gain_ref, sems.at[2]),
+        pltpu.make_async_copy(mod_hbm, mod_ref, sems.at[3]),
     ]
-    loads = []
-    for i in range(ROWS // STEP):
-        frame, row = divmod(i * STEP, TOK)
-        rows = pl.ds(row, STEP)
-        loads.append(
-            pltpu.make_async_copy(tok_hbm.at[frame, rows], tok_ref.at[frame, rows], sems.at[i])
-        )
+    loads = [pltpu.make_async_copy(tok_hbm.at[f], tok_ref.at[f], sems.at[f]) for f in range(2)]
     for copy in loads[:1] + side + loads[1:]:
         copy.start()
     for copy in side:
         copy.wait()
     for i in range(ROWS // STEP):
         frame, row = divmod(i * STEP, TOK)
-        loads[i].wait()
+        if row == 0:
+            loads[frame].wait()
         x = tok_ref[frame, row : row + STEP, :].astype(jnp.float32)
         meansq = jnp.mean(x * x, axis=-1, keepdims=True)
         scaled = x * lax.rsqrt(meansq + 1e-06) * gain_ref[...] * (1.0 + mod_ref[frame : frame + 1, :])
@@ -83,7 +78,7 @@
             pltpu.VMEM((2, TOK, D), jnp.bfloat16),
             pltpu.VMEM((1, D), jnp.float32),
             pltpu.VMEM((2, D), jnp.float32),
-            pltpu.SemaphoreType.DMA((ROWS // STEP + 2,)),
+            pltpu.SemaphoreType.DMA((4,)),
         ],
         compiler_params=params(8 << 20),
         cost_estimate=cost(ROWS * D * 8, ROWS * D * 6),
@@ -288,8 +283,8 @@
 
     def parts(frame, slots, masked):
         at = [slots(frame, b) for b in range(NBLK)]
-        for g in range(D // GW):
-            for b in range(NBLK):
+        for b in range(NBLK):
+            for g in range(D // GW):
                 where = (slice(b * BT, (b + 1) * BT), slice(g * GW, (g + 1) * GW))
                 yield where, part(frame, b, g, at[b], masked)
 

time: 43.7 us -> 43.1 us (0.986)
  Pallas kernels: 22.7 us -> 22 us
where the time goes in v5:
time: 43.1 us; the launch traced here: 42.5 us
  Pallas kernels  22 us (51%)
  starting transfers between devices  17.9 us (42%)
  waiting for transfers between devices  2.29 us (5%)
    ppermute x3, starting transfers between devices, forward(): return lax.ppermute(x, BOTH, onward)  15.5 us
    pallas_call x3, Pallas kernels, attend(): pl.pallas_call(functools.partial(attend_kernel, ats, finish), out_shape=o...  12.8 us
    pallas_call x1, Pallas kernels, own_project(): pl.pallas_call(functools.partial(own_kernel, n), out_shape=[jax.ShapeDtyp...  4.6 us
    pallas_call x2, Pallas kernels, kv_project(): pl.pallas_call(functools.partial(kv_kernel, ats, own), out_shape=[shape,...  3.2 us
    ppermute x3, starting transfers between devices, swap(): return lax.ppermute(x, BOTH, partner)  2.29 us
    ppermute x3, waiting for transfers between devices, swap(): return lax.ppermute(x, BOTH, partner)  2.28 us
    pallas_call x1, Pallas kernels, norm(): pl.pallas_call(norm_kernel, out_shape=[jax.ShapeDtypeStruct((ROWS, D), jn...  1.45 us
  transfers between devices with their start and end apart: 7, of which 1 were waited for; matrix products, arithmetic and copies ran while one was open for 0% of the time, Pallas kernels for 37%

profile of v5, /device:TPU:0, one launch (start us, length us, event | category | flops | bytes accessed | tf_op | source)
XLA Modules:
  0.0 42.5 jit_solution(6890650170218479853)
XLA Ops:
  0.0 1.4 %shard_map.100 = (bf16[384,1024]{1,0:T(8,128)(2,1)S(1)}, bf16[128,1024]{1,0:T(8,128)(2,1)S(1)}, bf16[128,1024]{1,0:T(8,128)(2,1)S(1)}, bf16[128,1024]{1,0:T(8,128)(2,1)S(1)}) custom-call(bf16[2,192,1024]{2,1,0:T(8,128)(2,1)} %tok_hbm.1, f32[1,1024]{1,0:T(1,128)} %bitcast.1, f32[2,1024]{1,0:T(2,128)} %mod_hbm.1), custom_call_target="tpu_custom_call" | custom-call | flops 3145728 | bytes 2359296 | tf_op jit(solution)/shard_map/pallas_call | solution.py:72
  1.5 0.1 collective-permute-start.3
  1.6 0.1 collective-permute-start.2
  1.7 2.0 %collective-permute-start.1 = (bf16[128,1024]{1,0:T(8,128)(2,1)S(1)}, bf16[128,1024]{1,0:T(8,128)(2,1)S(1)}, u32[]{:S(2)}, u32[]{:S(2)}) collective-permute-start(bf16[128,1024]{1,0:T(8,128)(2,1)S(1)} %get-tuple-element.32), channel_id=1, source_target_pairs={{0,128},{1,129},{2,130},{3,131},{4,132},{5,133},{6,134},{7,135},{8... | collective-permute-start | bytes 786440 | tf_op jit(solution)/shard_map/ppermute | solution.py:367
  3.7 0.0 copy-start.2
  3.7 0.0 copy-start.1
  3.7 4.6 %shard_map.101 = (bf16[128,1024]{1,0:T(8,128)(2,1)S(1)}, bf16[384,1024]{1,0:T(8,128)(2,1)S(1)}, bf16[384,1024]{1,0:T(8,128)(2,1)S(1)}, bf16[384,1024]{1,0:T(8,12...) custom-call(bf16[384,1024]{1,0:T(8,128)(2,1)S(1)} %get-tuple-element., ...), custom_call_target="tpu_custom_call", output_to_operand_aliasing={{0}: (4, {})} | custom-call | flops 2415919104 | bytes 6291456 | tf_op jit(solution)/shard_map/pallas_call | solution.py:112
  8.3 0.2 collective-permute-start
  8.5 0.0 copy-done.2
  8.5 0.0 copy-done.1
  8.5 2.3 %collective-permute-done.2.refs_0_ = bf16[128,1024]{1,0:T(8,128)(2,1)S(1)} collective-permute-done((bf16[128,1024]{1,0:T(8,128)(2,1)S(1)}, bf16[128,1024]{1,0:T(8,128)(2,1)S(1)}, u32[]{:S(2)}, u32[]{:S(2)}) %collective-permute-start.2) | collective-permute-done | bytes 262176 | tf_op jit(solution)/shard_map/ppermute | solution.py:367
  10.8 7.5 %collective-permute-start.5 = (bf16[128,1024]{1,0:T(8,128)(2,1)S(1)}, bf16[128,1024]{1,0:T(8,128)(2,1)S(1)}, u32[]{:S(2)}, u32[]{:S(2)}) collective-permute-start(bf16[128,1024]{1,0:T(8,128)(2,1)S(1)} %collective-permute-done.2.refs_0_), channel_id=1, source_target_pairs={{0,255},{1,130},{2,129},{3,132},{4,131},{5,134},{6,133},{7,136},{8... | collective-permute-start | bytes 786440 | tf_op jit(solution)/shard_map/ppermute | solution.py:373
  18.3 0.0 collective-permute-done.3.refs_1_
  18.3 2.5 %shard_map.102 = (bf16[1536,1024]{1,0:T(8,128)(2,1)S(1)}, bf16[1536,1024]{1,0:T(8,128)(2,1)S(1)}, f32[8,128]{1,0:T(8,128)S(1)}) custom-call(bf16[128,1024]{1,0:T(8,128)(2,1)S(1)} %collective-permute-done.2.refs_0_, bf16[384,1024]{1,0:T(8,128)(2,1)S(1)} %collective-permute-done.3.refs_1_, bf16[1024,1024]{1,0:T(8,128)(2,1)S(1)} %get-tuple-element.34.refs_2_.refs_1_, ...), custom_call_target="tpu_custom_call" | custom-call | flops 2147483648 | bytes 6291456 | tf_op jit(solution)/shard_map/pallas_call | solution.py:173
  20.8 0.0 collective-permute-done.1.refs_0_
  20.8 3.1 %collective-permute-start.6 = (bf16[128,1024]{1,0:T(8,128)(2,1)S(1)}, bf16[128,1024]{1,0:T(8,128)(2,1)S(1)}, u32[]{:S(2)}, u32[]{:S(2)}) collective-permute-start(bf16[128,1024]{1,0:T(8,128)(2,1)S(1)} %shard_map.103.refs_0_), channel_id=1, source_target_pairs={{0,255},{1,130},{2,129},{3,132},{4,131},{5,134},{6,133},{7,136},{8... | collective-permute-start | bytes 786440 | tf_op jit(solution)/shard_map/ppermute | solution.py:373
  23.9 0.0 copy-start
  23.9 0.7 %shard_map.104 = (bf16[1536,1024]{1,0:T(8,128)(2,1)S(1)}, bf16[1536,1024]{1,0:T(8,128)(2,1)S(1)}, f32[8,128]{1,0:T(8,128)S(1)}) custom-call(bf16[128,1024]{1,0:T(8,128)(2,1)S(1)} %shard_map.103.refs_0_, bf16[1024,1024]{1,0:T(8,128)(2,1)S(1)} %get-tuple-element.34.refs_2_.refs_1_, ...), custom_call_target="tpu_custom_call", output_to_operand_aliasing={{0}: (3, {}), {1}: (4, {})} | custom-call | flops 536870912 | bytes 6291456 | tf_op jit(solution)/shard_map/pallas_call | solution.py:173
  24.6 0.0 collective-permute-done.refs_0_
  24.7 4.9 %collective-permute-start.4 = (bf16[128,1024]{1,0:T(8,128)(2,1)S(1)}, bf16[128,1024]{1,0:T(8,128)(2,1)S(1)}, u32[]{:S(2)}, u32[]{:S(2)}) collective-permute-start(bf16[128,1024]{1,0:T(8,128)(2,1)S(1)} %shard_map.105.refs_0_), channel_id=1, source_target_pairs={{0,255},{1,130},{2,129},{3,132},{4,131},{5,134},{6,133},{7,136},{8... | collective-permute-start | bytes 786440 | tf_op jit(solution)/shard_map/ppermute | solution.py:373
  29.5 0.0 copy-done
  29.5 3.5 %shard_map.106 = (bf16[1536,1024]{1,0:T(8,128)(2,1)S(1)}, bf16[1536,1024]{1,0:T(8,128)(2,1)S(1)}, f32[2,192,1024]{2,1,0:T(8,128)S(1)}, f32[2,192,1024]{2,1,0:T(8,128)S(1)}) custom-call(bf16[128,1024]{1,0:T(8,128)(2,1)S(1)} %shard_map.105.refs_0_, ...), custom_call_target="tpu_custom_call", output_to_operand_aliasing={{0}: (7, {}), {1}: (8, {})} | custom-call | flops 2415919104 | bytes 8388608 | tf_op jit(solution)/shard_map/pallas_call | solution.py:343
  33.0 0.0 collective-permute-done.5.refs_0_
  33.0 0.0 collective-permute-done.6.refs_1_
  33.0 4.4 %shard_map.107 = (bf16[1536,1024]{1,0:T(8,128)(2,1)S(1)}, bf16[1536,1024]{1,0:T(8,128)(2,1)S(1)}, bf16[192,1024]{1,0:T(8,128)(2,1)S(1)}) custom-call(bf16[128,1024]{1,0:T(8,128)(2,1)S(1)} %collective-permute-done.5.refs_0_, bf16[128,1024]{1,0:T(8,128)(2,1)S(1)} %collective-permute-done.6.refs_1_, ...), custom_call_target="tpu_custom_call", output_to_operand_aliasing={{0}: (8, {}), {1}: (9, {})} | custom-call | flops 2415919104 | bytes 8388608 | tf_op jit(solution)/shard_map/pallas_call | solution.py:343
  37.5 0.0 collective-permute-done.4.refs_0_
  37.5 4.9 %shard_map.108 = (bf16[1536,1024]{1,0:T(8,128)(2,1)S(1)}, bf16[1536,1024]{1,0:T(8,128)(2,1)S(1)}, bf16[2,192,1024]{2,1,0:T(8,128)(2,1)}) custom-call(bf16[128,1024]{1,0:T(8,128)(2,1)S(1)} %collective-permute-done.4.refs_0_, bf16[1024,1024]{1,0:T(8,128)(2,1)S(1)} %get-tuple-element.34.refs_2_.refs_1_, ...), custom_call_target="tpu_custom_call", output_to_operand_aliasing={{0}: (7, {}), {1}: (8, {})} | custom-call | flops 2415919104 | bytes 8388608 | tf_op jit(solution)/shard_map/pallas_call | solution.py:343
  (4 shorter events, 0.0 us)
Async XLA Ops:
  1.5 16.8 %collective-permute-start.3 = (bf16[384,1024]{1,0:T(8,128)(2,1)S(1)}, bf16[384,1024]{1,0:T(8,128)(2,1)S(1)}, u32[]{:S(2)}, u32[]{:S(2)}) collective-permute-start(bf16[384,1024]{1,0:T(8,128)(2,1)S(1)} %get-tuple-element.29.refs_0_), channel_id=1, source_target_pairs={{0,1},{1,0},{2,3},{3,2},{4,5},{5,4},{6,7},{7,6},{8,9},{9,8},{10,11... | collective-permute-start | bytes 2359304 | tf_op jit(solution)/shard_map/ppermute | solution.py:370
  1.6 9.2 %collective-permute-start.2 = (bf16[128,1024]{1,0:T(8,128)(2,1)S(1)}, bf16[128,1024]{1,0:T(8,128)(2,1)S(1)}, u32[]{:S(2)}, u32[]{:S(2)}) collective-permute-start(bf16[128,1024]{1,0:T(8,128)(2,1)S(1)} %get-tuple-element.33), channel_id=1, source_target_pairs={{0,128},{1,129},{2,130},{3,131},{4,132},{5,133},{6,134},{7,135},{8... | collective-permute-start | bytes 786440 | tf_op jit(solution)/shard_map/ppermute | solution.py:367
  1.7 19.1 %collective-permute-start.1 = (bf16[128,1024]{1,0:T(8,128)(2,1)S(1)}, bf16[128,1024]{1,0:T(8,128)(2,1)S(1)}, u32[]{:S(2)}, u32[]{:S(2)}) collective-permute-start(bf16[128,1024]{1,0:T(8,128)(2,1)S(1)} %get-tuple-element.32), channel_id=1, source_target_pairs={{0,128},{1,129},{2,130},{3,131},{4,132},{5,133},{6,134},{7,135},{8... | collective-permute-start | bytes 786440 | tf_op jit(solution)/shard_map/ppermute | solution.py:367
  3.7 4.8 %copy-start.2 = (s32[1,3,6]{2,0,1:T(1,128)S(1)}, s32[1,3,6]{2,0,1:T(1,128)}, u32[]{:S(2)}) copy-start(s32[1,3,6]{2,0,1:T(1,128)} %param.17) | copy-start | bytes 220
  3.7 4.8 %copy-start.1 = (s32[2,1,3,4]{3,1,2,0:T(1,128)S(1)}, s32[2,1,3,4]{3,1,2,0:T(1,128)}, u32[]{:S(2)}) copy-start(s32[2,1,3,4]{3,1,2,0:T(1,128)} %param.19) | copy-start | bytes 292
  8.3 16.4 %collective-permute-start = (bf16[128,1024]{1,0:T(8,128)(2,1)S(1)}, bf16[128,1024]{1,0:T(8,128)(2,1)S(1)}, u32[]{:S(2)}, u32[]{:S(2)}) collective-permute-start(bf16[128,1024]{1,0:T(8,128)(2,1)S(1)} %get-tuple-element.31), channel_id=1, source_target_pairs={{0,128},{1,129},{2,130},{3,131},{4,132},{5,133},{6,134},{7,135},{8... | collective-permute-start | bytes 786440 | tf_op jit(solution)/shard_map/ppermute | solution.py:367
  10.8 22.3 %collective-permute-start.5 = (bf16[128,1024]{1,0:T(8,128)(2,1)S(1)}, bf16[128,1024]{1,0:T(8,128)(2,1)S(1)}, u32[]{:S(2)}, u32[]{:S(2)}) collective-permute-start(bf16[128,1024]{1,0:T(8,128)(2,1)S(1)} %collective-permute-done.2.refs_0_), channel_id=1, source_target_pairs={{0,255},{1,130},{2,129},{3,132},{4,131},{5,134},{6,133},{7,136},{8... | collective-permute-start | bytes 786440 | tf_op jit(solution)/shard_map/ppermute | solution.py:373
  20.8 12.2 %collective-permute-start.6 = (bf16[128,1024]{1,0:T(8,128)(2,1)S(1)}, bf16[128,1024]{1,0:T(8,128)(2,1)S(1)}, u32[]{:S(2)}, u32[]{:S(2)}) collective-permute-start(bf16[128,1024]{1,0:T(8,128)(2,1)S(1)} %shard_map.103.refs_0_), channel_id=1, source_target_pairs={{0,255},{1,130},{2,129},{3,132},{4,131},{5,134},{6,133},{7,136},{8... | collective-permute-start | bytes 786440 | tf_op jit(solution)/shard_map/ppermute | solution.py:373
  23.9 5.6 %copy-start = (s32[1,3]{1,0:T(1,128)S(1)}, s32[1,3]{1,0:T(1,128)}, u32[]{:S(2)}) copy-start(s32[1,3]{1,0:T(1,128)} %refs_5_.4) | copy-start | bytes 40
  24.7 12.8 %collective-permute-start.4 = (bf16[128,1024]{1,0:T(8,128)(2,1)S(1)}, bf16[128,1024]{1,0:T(8,128)(2,1)S(1)}, u32[]{:S(2)}, u32[]{:S(2)}) collective-permute-start(bf16[128,1024]{1,0:T(8,128)(2,1)S(1)} %shard_map.105.refs_0_), channel_id=1, source_target_pairs={{0,255},{1,130},{2,129},{3,132},{4,131},{5,134},{6,133},{7,136},{8... | collective-permute-start | bytes 786440 | tf_op jit(solution)/shard_map/ppermute | solution.py:373

commit v6 on v5

--- a/solution.py
+++ b/solution.py
@@ -194,12 +194,12 @@
     wk_ref, wv_ref, q_ref, neigh_hbm, count_hbm, cross_hbm = take(6)
     take(2)
     if finish is not None:
-        part_refs, (wo_hbm,) = take(2), take(1)
+        part_refs, (wo_hbm,) = take(3), take(1)
     if finish == 1:
         (first_ref,) = take(1)
     k_ref, v_ref = take(2)
     if finish is None:
-        part_refs = take(2)
+        part_refs = take(3)
     else:
         (out_ref,) = take(1)
     neigh_ref, count_ref, cross_ref, sems = take(4)
@@ -292,13 +292,13 @@
         for frame in range(2):
             for where, values in parts(frame, far_slots, False):
                 att, peak, total = values
-                part_refs[0][(frame, *where)] = att / total
-                part_refs[1][(frame, *where)] = peak * EXP_SCALE + jnp.log2(total)
+                for ref, value in zip(part_refs, (att, peak, total)):
+                    ref[(frame, *where)] = value
         return
     for where, (att, peak, total) in parts(finish, near_slots, True):
-        far, level = (ref[(finish, *where)] for ref in part_refs)
-        scale = jnp.exp2(jnp.minimum(peak * EXP_SCALE - level, FAR_AHEAD))
-        att_ref[where] = ((far + att * scale) / (1.0 + total * scale)).astype(jnp.bfloat16)
+        att2, peak2, total2 = (ref[(finish, *where)] for ref in part_refs)
+        scale = jnp.exp2(jnp.minimum((peak - peak2) * EXP_SCALE, FAR_AHEAD))
+        att_ref[where] = ((att2 + att * scale) / (total2 + total * scale)).astype(jnp.bfloat16)
     wo_copy.wait()
     if finish == 0:
         project_into(att_ref[...], wo_ref, out_ref, 0)
@@ -325,11 +325,11 @@
     scratch = [pltpu.SMEM(x.shape, jnp.int32) for x in lists] + [pltpu.SemaphoreType.DMA((9,))]
     rows = pltpu.VMEM((TOK, D), jnp.bfloat16)
     if finish is None:
-        out_shape += [jax.ShapeDtypeStruct((2, TOK, D), jnp.float32)] * 2
-        out_specs += [VMEM] * 2
+        out_shape += [jax.ShapeDtypeStruct((2, TOK, D), jnp.float32)] * 3
+        out_specs += [VMEM] * 3
     else:
         args += [*parts, in_hbm(w_out)]
-        in_specs += [VMEM] * 2 + [ANY]
+        in_specs += [VMEM] * 3 + [ANY]
         scratch += [pltpu.VMEM((D, D), jnp.bfloat16), rows]
     if finish == 0:
         out_shape.append(rows)
@@ -388,9 +388,9 @@
     *held, token = kv_project([s1], [at(1, 1)], wk, wv, held, False)
     s2 = gate(s2, token)
     o2 = forward(s2)
-    *held, far, level = attend([s2], [at(1, 2)], wk, wv, held, queries, lists)
-    parts = far, level
-    *held, first = attend([o0, o1], [at(3, 0), at(3, 1)], wk, wv, held, queries, lists, 0, parts, w_out)
+    *held, att, peak, total = attend([s2, o0], [at(1, 2), at(3, 0)], wk, wv, held, queries, lists)
+    parts = att, peak, total
+    *held, first = attend([o1], [at(3, 1)], wk, wv, held, queries, lists, 0, parts, w_out)
     return attend([o2], [at(3, 2)], wk, wv, held, queries, lists, 1, parts, w_out, first)[2]
 
 

time: 43.1 us -> 42.7 us (level)
  no operation moved by 1% of the time
where the time goes in v6:
time: 42.7 us; the launch traced here: 42.2 us
  Pallas kernels  21.7 us (51%)
  starting transfers between devices  17.9 us (42%)
  waiting for transfers between devices  2.29 us (5%)
    ppermute x3, starting transfers between devices, forward(): return lax.ppermute(x, BOTH, onward)  15.5 us
    pallas_call x3, Pallas kernels, attend(): pl.pallas_call(functools.partial(attend_kernel, ats, finish), out_shape=o...  12.4 us
    pallas_call x1, Pallas kernels, own_project(): pl.pallas_call(functools.partial(own_kernel, n), out_shape=[jax.ShapeDtyp...  4.6 us
    pallas_call x2, Pallas kernels, kv_project(): pl.pallas_call(functools.partial(kv_kernel, ats, own), out_shape=[shape,...  3.2 us
    ppermute x3, starting transfers between devices, swap(): return lax.ppermute(x, BOTH, partner)  2.3 us
    ppermute x3, waiting for transfers between devices, swap(): return lax.ppermute(x, BOTH, partner)  2.28 us
    pallas_call x1, Pallas kernels, norm(): pl.pallas_call(norm_kernel, out_shape=[jax.ShapeDtypeStruct((ROWS, D), jn...  1.45 us
  transfers between devices with their start and end apart: 7, of which 1 were waited for; matrix products, arithmetic and copies ran while one was open for 0% of the time, Pallas kernels for 37%

profile of v6, /device:TPU:0, one launch (start us, length us, event | category | flops | bytes accessed | tf_op | source)
XLA Modules:
  0.0 42.2 jit_solution(15217133677073757375)
XLA Ops:
  0.0 1.4 %shard_map.100 = (bf16[384,1024]{1,0:T(8,128)(2,1)S(1)}, bf16[128,1024]{1,0:T(8,128)(2,1)S(1)}, bf16[128,1024]{1,0:T(8,128)(2,1)S(1)}, bf16[128,1024]{1,0:T(8,128)(2,1)S(1)}) custom-call(bf16[2,192,1024]{2,1,0:T(8,128)(2,1)} %tok_hbm.1, f32[1,1024]{1,0:T(1,128)} %bitcast.1, f32[2,1024]{1,0:T(2,128)} %mod_hbm.1), custom_call_target="tpu_custom_call" | custom-call | flops 3145728 | bytes 2359296 | tf_op jit(solution)/shard_map/pallas_call | solution.py:72
  1.5 0.1 collective-permute-start.3
  1.6 0.1 collective-permute-start.2
  1.7 2.0 %collective-permute-start.1 = (bf16[128,1024]{1,0:T(8,128)(2,1)S(1)}, bf16[128,1024]{1,0:T(8,128)(2,1)S(1)}, u32[]{:S(2)}, u32[]{:S(2)}) collective-permute-start(bf16[128,1024]{1,0:T(8,128)(2,1)S(1)} %get-tuple-element.33), channel_id=1, source_target_pairs={{0,128},{1,129},{2,130},{3,131},{4,132},{5,133},{6,134},{7,135},{8... | collective-permute-start | bytes 786440 | tf_op jit(solution)/shard_map/ppermute | solution.py:367
  3.7 0.0 copy-start.2
  3.7 0.0 copy-start.1
  3.7 4.6 %shard_map.101 = (bf16[128,1024]{1,0:T(8,128)(2,1)S(1)}, bf16[384,1024]{1,0:T(8,128)(2,1)S(1)}, bf16[384,1024]{1,0:T(8,128)(2,1)S(1)}, bf16[384,1024]{1,0:T(8,12...) custom-call(bf16[384,1024]{1,0:T(8,128)(2,1)S(1)} %get-tuple-element., ...), custom_call_target="tpu_custom_call", output_to_operand_aliasing={{0}: (4, {})} | custom-call | flops 2415919104 | bytes 6291456 | tf_op jit(solution)/shard_map/pallas_call | solution.py:112
  8.3 0.2 collective-permute-start
  8.5 2.3 %collective-permute-done.2.refs_0_ = bf16[128,1024]{1,0:T(8,128)(2,1)S(1)} collective-permute-done((bf16[128,1024]{1,0:T(8,128)(2,1)S(1)}, bf16[128,1024]{1,0:T(8,128)(2,1)S(1)}, u32[]{:S(2)}, u32[]{:S(2)}) %collective-permute-start.2) | collective-permute-done | bytes 262176 | tf_op jit(solution)/shard_map/ppermute | solution.py:367
  10.8 7.5 %collective-permute-start.6 = (bf16[128,1024]{1,0:T(8,128)(2,1)S(1)}, bf16[128,1024]{1,0:T(8,128)(2,1)S(1)}, u32[]{:S(2)}, u32[]{:S(2)}) collective-permute-start(bf16[128,1024]{1,0:T(8,128)(2,1)S(1)} %collective-permute-done.2.refs_0_), channel_id=1, source_target_pairs={{0,255},{1,130},{2,129},{3,132},{4,131},{5,134},{6,133},{7,136},{8... | collective-permute-start | bytes 786440 | tf_op jit(solution)/shard_map/ppermute | solution.py:373
  18.3 0.0 copy-done.2
  18.3 0.0 copy-done.1
  18.3 0.0 collective-permute-done.3.refs_1_
  18.3 2.5 %shard_map.102 = (bf16[1536,1024]{1,0:T(8,128)(2,1)S(1)}, bf16[1536,1024]{1,0:T(8,128)(2,1)S(1)}, f32[8,128]{1,0:T(8,128)S(1)}) custom-call(bf16[128,1024]{1,0:T(8,128)(2,1)S(1)} %collective-permute-done.2.refs_0_, bf16[384,1024]{1,0:T(8,128)(2,1)S(1)} %collective-permute-done.3.refs_1_, bf16[1024,1024]{1,0:T(8,128)(2,1)S(1)} %get-tuple-element.35.refs_2_.refs_1_, ...), custom_call_target="tpu_custom_call" | custom-call | flops 2147483648 | bytes 6291456 | tf_op jit(solution)/shard_map/pallas_call | solution.py:173
  20.8 0.0 collective-permute-done.1.refs_0_
  20.8 3.1 %collective-permute-start.5 = (bf16[128,1024]{1,0:T(8,128)(2,1)S(1)}, bf16[128,1024]{1,0:T(8,128)(2,1)S(1)}, u32[]{:S(2)}, u32[]{:S(2)}) collective-permute-start(bf16[128,1024]{1,0:T(8,128)(2,1)S(1)} %shard_map.103.refs_0_), channel_id=1, source_target_pairs={{0,255},{1,130},{2,129},{3,132},{4,131},{5,134},{6,133},{7,136},{8... | collective-permute-start | bytes 786440 | tf_op jit(solution)/shard_map/ppermute | solution.py:373
  23.9 0.0 copy-start
  23.9 0.7 %shard_map.104 = (bf16[1536,1024]{1,0:T(8,128)(2,1)S(1)}, bf16[1536,1024]{1,0:T(8,128)(2,1)S(1)}, f32[8,128]{1,0:T(8,128)S(1)}) custom-call(bf16[128,1024]{1,0:T(8,128)(2,1)S(1)} %shard_map.103.refs_0_, bf16[1024,1024]{1,0:T(8,128)(2,1)S(1)} %get-tuple-element.35.refs_2_.refs_1_, ...), custom_call_target="tpu_custom_call", output_to_operand_aliasing={{0}: (3, {}), {1}: (4, {})} | custom-call | flops 536870912 | bytes 6291456 | tf_op jit(solution)/shard_map/pallas_call | solution.py:173
  24.6 0.0 collective-permute-done.refs_0_
  24.7 4.9 %collective-permute-start.4 = (bf16[128,1024]{1,0:T(8,128)(2,1)S(1)}, bf16[128,1024]{1,0:T(8,128)(2,1)S(1)}, u32[]{:S(2)}, u32[]{:S(2)}) collective-permute-start(bf16[128,1024]{1,0:T(8,128)(2,1)S(1)} %shard_map.105.refs_0_), channel_id=1, source_target_pairs={{0,255},{1,130},{2,129},{3,132},{4,131},{5,134},{6,133},{7,136},{8... | collective-permute-start | bytes 786440 | tf_op jit(solution)/shard_map/ppermute | solution.py:373
  29.5 0.0 collective-permute-done.6.refs_1_
  29.5 0.0 copy-done
  29.5 3.6 %shard_map.106 = (bf16[1536,1024]{1,0:T(8,128)(2,1)S(1)}, bf16[1536,1024]{1,0:T(8,128)(2,1)S(1)}, f32[2,192,1024]{2,1,0:T(8,128)S(1)}, f32[2,192,1024]{2,1,0:T(8,128)S(1)}, f32[2,192,1024]{2,1,0:T(8,128)S(1)}) custom-call(bf16[128,1024]{1,0:T(8,128)(2,1)S(1)} %shard_map.105.refs_0_, ...), custom_call_target="tpu_custom_call", output_to_operand_aliasing={{0}: (8, {}), {1}: (9, {})} | custom-call | flops 2415919104 | bytes 8388608 | tf_op jit(solution)/shard_map/pallas_call | solution.py:343
  33.1 0.0 collective-permute-done.5.refs_0_
  33.1 4.2 %shard_map.107 = (bf16[1536,1024]{1,0:T(8,128)(2,1)S(1)}, bf16[1536,1024]{1,0:T(8,128)(2,1)S(1)}, bf16[192,1024]{1,0:T(8,128)(2,1)S(1)}) custom-call(bf16[128,1024]{1,0:T(8,128)(2,1)S(1)} %collective-permute-done.5.refs_0_, bf16[1024,1024]{1,0:T(8,128)(2,1)S(1)} %get-tuple-element.35.refs_2_.refs_1_, ...), custom_call_target="tpu_custom_call", output_to_operand_aliasing={{0}: (7, {}), {1}: (8, {})} | custom-call | flops 2415919104 | bytes 8388608 | tf_op jit(solution)/shard_map/pallas_call | solution.py:343
  37.3 0.0 collective-permute-done.4.refs_0_
  37.4 4.6 %shard_map.108 = (bf16[1536,1024]{1,0:T(8,128)(2,1)S(1)}, bf16[1536,1024]{1,0:T(8,128)(2,1)S(1)}, bf16[2,192,1024]{2,1,0:T(8,128)(2,1)}) custom-call(bf16[128,1024]{1,0:T(8,128)(2,1)S(1)} %collective-permute-done.4.refs_0_, bf16[1024,1024]{1,0:T(8,128)(2,1)S(1)} %get-tuple-element.35.refs_2_.refs_1_, ...), custom_call_target="tpu_custom_call", output_to_operand_aliasing={{0}: (7, {}), {1}: (8, {})} | custom-call | flops 2415919104 | bytes 8388608 | tf_op jit(solution)/shard_map/pallas_call | solution.py:343
  (4 shorter events, 0.0 us)
Async XLA Ops:
  1.5 16.9 %collective-permute-start.3 = (bf16[384,1024]{1,0:T(8,128)(2,1)S(1)}, bf16[384,1024]{1,0:T(8,128)(2,1)S(1)}, u32[]{:S(2)}, u32[]{:S(2)}) collective-permute-start(bf16[384,1024]{1,0:T(8,128)(2,1)S(1)} %get-tuple-element.30.refs_0_), channel_id=1, source_target_pairs={{0,1},{1,0},{2,3},{3,2},{4,5},{5,4},{6,7},{7,6},{8,9},{9,8},{10,11... | collective-permute-start | bytes 2359304 | tf_op jit(solution)/shard_map/ppermute | solution.py:370
  1.6 9.2 %collective-permute-start.2 = (bf16[128,1024]{1,0:T(8,128)(2,1)S(1)}, bf16[128,1024]{1,0:T(8,128)(2,1)S(1)}, u32[]{:S(2)}, u32[]{:S(2)}) collective-permute-start(bf16[128,1024]{1,0:T(8,128)(2,1)S(1)} %get-tuple-element.34), channel_id=1, source_target_pairs={{0,128},{1,129},{2,130},{3,131},{4,132},{5,133},{6,134},{7,135},{8... | collective-permute-start | bytes 786440 | tf_op jit(solution)/shard_map/ppermute | solution.py:367
  1.7 19.1 %collective-permute-start.1 = (bf16[128,1024]{1,0:T(8,128)(2,1)S(1)}, bf16[128,1024]{1,0:T(8,128)(2,1)S(1)}, u32[]{:S(2)}, u32[]{:S(2)}) collective-permute-start(bf16[128,1024]{1,0:T(8,128)(2,1)S(1)} %get-tuple-element.33), channel_id=1, source_target_pairs={{0,128},{1,129},{2,130},{3,131},{4,132},{5,133},{6,134},{7,135},{8... | collective-permute-start | bytes 786440 | tf_op jit(solution)/shard_map/ppermute | solution.py:367
  3.7 14.6 %copy-start.2 = (s32[1,3,6]{2,0,1:T(1,128)S(1)}, s32[1,3,6]{2,0,1:T(1,128)}, u32[]{:S(2)}) copy-start(s32[1,3,6]{2,0,1:T(1,128)} %param.17) | copy-start | bytes 220
  3.7 14.6 %copy-start.1 = (s32[2,1,3,4]{3,1,2,0:T(1,128)S(1)}, s32[2,1,3,4]{3,1,2,0:T(1,128)}, u32[]{:S(2)}) copy-start(s32[2,1,3,4]{3,1,2,0:T(1,128)} %param.19) | copy-start | bytes 292
  8.3 16.4 %collective-permute-start = (bf16[128,1024]{1,0:T(8,128)(2,1)S(1)}, bf16[128,1024]{1,0:T(8,128)(2,1)S(1)}, u32[]{:S(2)}, u32[]{:S(2)}) collective-permute-start(bf16[128,1024]{1,0:T(8,128)(2,1)S(1)} %get-tuple-element.32), channel_id=1, source_target_pairs={{0,128},{1,129},{2,130},{3,131},{4,132},{5,133},{6,134},{7,135},{8... | collective-permute-start | bytes 786440 | tf_op jit(solution)/shard_map/ppermute | solution.py:367
  10.8 18.8 %collective-permute-start.6 = (bf16[128,1024]{1,0:T(8,128)(2,1)S(1)}, bf16[128,1024]{1,0:T(8,128)(2,1)S(1)}, u32[]{:S(2)}, u32[]{:S(2)}) collective-permute-start(bf16[128,1024]{1,0:T(8,128)(2,1)S(1)} %collective-permute-done.2.refs_0_), channel_id=1, source_target_pairs={{0,255},{1,130},{2,129},{3,132},{4,131},{5,134},{6,133},{7,136},{8... | collective-permute-start | bytes 786440 | tf_op jit(solution)/shard_map/ppermute | solution.py:373
  20.8 12.3 %collective-permute-start.5 = (bf16[128,1024]{1,0:T(8,128)(2,1)S(1)}, bf16[128,1024]{1,0:T(8,128)(2,1)S(1)}, u32[]{:S(2)}, u32[]{:S(2)}) collective-permute-start(bf16[128,1024]{1,0:T(8,128)(2,1)S(1)} %shard_map.103.refs_0_), channel_id=1, source_target_pairs={{0,255},{1,130},{2,129},{3,132},{4,131},{5,134},{6,133},{7,136},{8... | collective-permute-start | bytes 786440 | tf_op jit(solution)/shard_map/ppermute | solution.py:373
  23.9 5.6 %copy-start = (s32[1,3]{1,0:T(1,128)S(1)}, s32[1,3]{1,0:T(1,128)}, u32[]{:S(2)}) copy-start(s32[1,3]{1,0:T(1,128)} %refs_5_.4) | copy-start | bytes 40
  24.7 12.7 %collective-permute-start.4 = (bf16[128,1024]{1,0:T(8,128)(2,1)S(1)}, bf16[128,1024]{1,0:T(8,128)(2,1)S(1)}, u32[]{:S(2)}, u32[]{:S(2)}) collective-permute-start(bf16[128,1024]{1,0:T(8,128)(2,1)S(1)} %shard_map.105.refs_0_), channel_id=1, source_target_pairs={{0,255},{1,130},{2,129},{3,132},{4,131},{5,134},{6,133},{7,136},{8... | collective-permute-start | bytes 786440 | tf_op jit(solution)/shard_map/ppermute | solution.py:373
